TPU v7x, 256 devices: a whole 4x4x8 slice. The times are simulated.
256 devices in a mesh: row: 64 (over y, x_lo, z), col: 4 (over x_hi, core).
Axes of the slice: x: 4 (x_hi: 2, x_lo: 2; x = x_hi * 2 + x_lo), y: 4, z: 8, core: 2. Of those that a mesh axis runs over, the one named last changes fastest.
Arguments:
- amplitudes: bfloat16 [128, 1024, 1200], P(None, 'row', 'col'), may hold values from -16 to 16
- integrals: bfloat16 [128, 1200, 4800], P('row', None, 'col'), may hold values from -0.046875 to 0.046875
- occupied_irrep: int32 [128], replicated, may hold values from 0 to 7
- virtual_irrep: int32 [1200], replicated, may hold values from 0 to 7, as said below
- occupied_energy: float32 [128], replicated, may hold values from -1.2 to -0.3
- virtual_energy: float32 [1200], replicated, may hold values from 0.1 to 1.5
- residual_in: float32 [1024, 4800], P('row', 'col'), may hold values from -6 to 6
Outputs:
- update: float32 [1024, 4800], P('row', 'col')
Inputs may be any that keep to these rules, and one draw needn't show every extreme that they name: `occupied_irrep`: D2h irrep labels. `virtual_irrep`: D2h irrep labels, never decreasing along the orbitals; each label is held by 1 to 200 orbitals, one label by exactly 200.
All inputs are finite; a program needn't handle non-finite values.
Results may differ from a plain program's by a relative error of at most 0.0003.
Values may be sent and summed in bfloat16 or wider, within the bound.
No kernel may reach another device: no remote copies, remote signals or barrier semaphores. Data moves between devices by JAX's collectives and lax.ppermute only.
A program may use at most 64 MiB of HBM per device.

v0:
```python
import jax
import jax.numpy as jnp
from jax import lax
from jax.sharding import PartitionSpec as P

NJ = 4


def local(
    amplitudes,
    integrals,
    occupied_irrep,
    virtual_irrep,
    occupied_energy,
    virtual_energy,
    residual_in,
):
    widened = lax.all_gather(amplitudes, "col", axis=2, tiled=True)
    arrived = lax.all_to_all(widened, "row", split_axis=0, concat_axis=1, tiled=True)
    occ_local = integrals.shape[0]
    cols_local = integrals.shape[2]
    rows_local = residual_in.shape[0]
    k_labels = lax.dynamic_slice_in_dim(
        occupied_irrep, lax.axis_index("row") * occ_local, occ_local
    )
    a_labels = virtual_irrep[: arrived.shape[1]]
    i_label = occupied_irrep[0]
    keep_amp = (
        jnp.bitwise_xor(
            jnp.bitwise_xor(i_label, k_labels)[:, None, None],
            jnp.bitwise_xor(a_labels[:, None], virtual_irrep[None, :])[None, :, :],
        )
        == 0
    )
    sym_amplitudes = jnp.where(keep_amp, arrived, jnp.zeros_like(arrived))
    col_start = lax.axis_index("col") * cols_local
    jb_labels = jnp.bitwise_xor(
        occupied_irrep[1 : 1 + NJ][:, None], virtual_irrep[None, :]
    ).reshape(-1)
    jb_local = lax.dynamic_slice_in_dim(jb_labels, col_start, cols_local)
    keep_int = (
        jnp.bitwise_xor(
            jnp.bitwise_xor(k_labels[:, None, None], virtual_irrep[None, :, None]),
            jb_local[None, None, :],
        )
        == 0
    )
    sym_integrals = jnp.where(keep_int, integrals, jnp.zeros_like(integrals))
    cycle_term = lax.psum_scatter(
        jnp.einsum(
            "kac,kcn->an", sym_amplitudes, sym_integrals, preferred_element_type=jnp.float32
        ),
        "row",
        scatter_dimension=0,
        tiled=True,
    )
    energy_a = lax.dynamic_slice_in_dim(
        virtual_energy, lax.axis_index("row") * rows_local, rows_local
    )
    energy_jb = (occupied_energy[1 : 1 + NJ][:, None] - virtual_energy[None, :]).reshape(-1)
    energy_local = lax.dynamic_slice_in_dim(energy_jb, col_start, cols_local)
    denominator = occupied_energy[0] - energy_a[:, None] + energy_local[None, :]
    return (residual_in + cycle_term) / denominator


def solution(mesh):
    in_specs = (P(None, "row", "col"), P("row", None, "col"), P(), P(), P(), P(), P("row", "col"))
    out_specs = P("row", "col")
    return jax.shard_map(local, mesh=mesh, in_specs=in_specs, out_specs=out_specs, check_vma=False)
```

profile of v0, /device:TPU:4, one launch (start us, length us, event | category | flops | bytes accessed | tf_op | source)
XLA Modules:
  0.0 542.0 jit_solution(12766070409721841654)
XLA Ops:
  6.5 0.0 all-gather.2.cloned.1.call-start
  6.5 0.7 all-gather.2.cloned.1.call-update
  7.3 47.4 %all-gather.2.cloned.1.call-done = bf16[128,16,1200]{0,1,2:T(8,128)(2,1)} async-done(((bf16[128,16,300]{0,1,2:T(8,128)(2,1)}), bf16[128,16,1200]{0,1,2:T(8,128)(2,1)}) %all-gather.2.cloned.1.call-update) | async-done | bytes 4915216 | tf_op jit(solution)/shard_map/all_gather | solution.py:18
  54.6 9.4 %copy.12 = bf16[128,16,1200]{2,1,0:T(8,128)(2,1)} copy(bf16[128,16,1200]{0,1,2:T(8,128)(2,1)} %all-gather.2.cloned.1.call-done) | data formatting | bytes 9830400 | tf_op jit(solution)/shard_map/all_gather | solution.py:18
  64.0 0.0 copy-start.4
  64.0 12.6 %all-to-all-start = ((bf16[128,16,1200]{2,1,0:T(8,128)(2,1)}), bf16[128,16,1200]{2,1,0:T(8,128)(2,1)}, u32[]{:S(2)}, u32[]{:S(2)}) async-start(bf16[128,16,1200]{2,1,0:T(8,128)(2,1)} %copy.12), calls=%async_computation | async-start | bytes 10485760 | tf_op jit(solution)/shard_map/all_to_all | solution.py:19
  76.6 0.0 reduce-scatter.2.cloned.1.call-start
  76.7 0.0 copy-done.4
  76.7 0.1 slice.17
  76.8 0.0 copy-done.1
  76.8 0.1 broadcast_xor_fusion.1
  76.9 0.1 xor.99
  77.0 0.1 dynamic_slice.13
  77.0 0.1 broadcast_xor_fusion.3
  77.1 0.1 broadcast_xor_fusion.2
  77.2 0.0 slice-done
  77.2 2.8 broadcast_xor_fusion
  80.0 116.0 %all-to-all-done = bf16[128,16,1200]{2,1,0:T(8,128)(2,1)} async-done(((bf16[128,16,1200]{2,1,0:T(8,128)(2,1)}), bf16[128,16,1200]{2,1,0:T(8,128)(2,1)}, u32[]{:S(2)}, u32[]{:S(2)}) %all-to-all-start) | async-done | bytes 4915232 | tf_op jit(solution)/shard_map/all_to_all | solution.py:19
  196.0 3.0 copy.13
  199.0 1.1 copy-done
  200.1 12.8 %fusion.11 = f32[1024,1200]{1,0:T(8,128)} fusion(bf16[2,1200,1200]{2,1,0:T(8,128)(2,1)} %param.8, s32[1200]{0:T(1024)S(1)} %dynamic_slice.13, s32[2,1200]{1,0:T(2,128)S(1)} %broadcast_xor_fusion.2, bf16[2,1024,1200]{2,1,0:T(8,128)(2,1)S(1)} %bitcast.10, s32[1024,1200]{1,0:T(8,128)S(1)} %copy-done, s32[2]{0:T(128)S(1)} %get-tuple-element.5), kind=kOutput, calls=%fused_computation.11 | convolution fusion | flops 5914252800 | bytes 20520008 | tf_op jit(solution)/shard_map/kac,kcn->an/dot_general | solution.py:50
  212.9 0.0 reduce-scatter.2.cloned.1.call-update
  212.9 0.6 copy-done.5
  213.5 0.1 slice.19
  213.6 0.0 copy-done.3
  213.6 0.1 broadcast_subtract_fusion
  213.7 0.1 sub.29
  213.8 0.1 dynamic_slice.15
  213.8 0.1 dynamic-slice_subtract_fusion
  213.9 319.6 %reduce-scatter.2.cloned.1.call-done = f32[16,1200]{1,0:T(8,128)} async-done(((f32[1024,1200]{1,0:T(8,128)}), f32[16,1200]{1,0:T(8,128)}) %reduce-scatter.2.cloned.1.call-update) | async-done | bytes 76816 | tf_op jit(solution)/shard_map/reduce_scatter | solution.py:49
  533.6 0.0 copy-done.2
  533.6 1.6 add_divide_fusion
  (6 shorter events, 0.0 us)
Async XLA Ops:
  6.5 48.1 %all-gather.2.cloned.1.call-start = ((), (), s32[]{:S(2)}) async-start(), calls=%async_computation.2 | async-start | bytes 6144000 | tf_op jit(solution)/shard_map/all_gather | solution.py:18
  64.0 12.7 %copy-start.4 = (s32[128]{0:T(128)S(1)}, s32[128]{0:T(128)}, u32[]{:S(2)}) copy-start(s32[128]{0:T(128)} %param.9) | copy-start | bytes 1540
  64.0 12.7 %copy-start.1 = (s32[1200]{0:T(1024)S(1)}, s32[1200]{0:T(1024)}, u32[]{:S(2)}) copy-start(s32[1200]{0:T(1024)} %param.10) | copy-start | bytes 14404
  64.0 13.2 %slice-start = ((s32[1200]{0:T(1024)}), s32[1024]{0:T(1024)S(1)}, s32[]{:S(2)}) async-start(s32[1200]{0:T(1024)} %param.10), calls=%async_computation.4 | async-start | bytes 8192 | tf_op jit(solution)/shard_map/slice | solution.py:26
  64.0 132.0 %all-to-all-start = ((bf16[128,16,1200]{2,1,0:T(8,128)(2,1)}), bf16[128,16,1200]{2,1,0:T(8,128)(2,1)}, u32[]{:S(2)}, u32[]{:S(2)}) async-start(bf16[128,16,1200]{2,1,0:T(8,128)(2,1)} %copy.12), calls=%async_computation | async-start | bytes 10485760 | tf_op jit(solution)/shard_map/all_to_all | solution.py:19
  76.6 457.0 %reduce-scatter.2.cloned.1.call-start = ((), (), s32[]{:S(2)}) async-start(), calls=%async_computation.3 | async-start | bytes 5324800 | tf_op jit(solution)/shard_map/reduce_scatter | solution.py:49
  196.0 4.0 copy-start
  212.9 0.7 copy-start.5
  212.9 0.7 copy-start.3
  212.9 320.7 %copy-start.2 = (f32[16,1200]{1,0:T(8,128)S(1)}, f32[16,1200]{1,0:T(8,128)}, u32[]{:S(2)}) copy-start(f32[16,1200]{1,0:T(8,128)} %param.13) | copy-start | bytes 230404
Sparse Core Ops, SparseCore 0:
  9.2 45.4 all-gather.1
  213.0 320.5 reduce-scatter.1
where the time goes:
time: 542 us
  waiting for transfers between devices  484 us (89%)
  local copies, waits for them, and re-layouts  14.6 us (3%)
  between operations  13.5 us (2%)
  matrix products  12.8 us (2%)
  starting transfers between devices  12.6 us (2%)
    reduce_scatter x1, waiting for transfers between devices, local(): lax.psum_scatter(jnp.einsum('kac,kcn->an', sym_amplitudes, sym_integrals,...  320 us
    all_to_all x1, waiting for transfers between devices, local(): lax.all_to_all(widened, 'row', split_axis=0, concat_axis=1, tiled=True)  116 us
    all_gather x1, waiting for transfers between devices, local(): widened = lax.all_gather(amplitudes, 'col', axis=2, tiled=True)  47.4 us
    dot_general x1, matrix products, local(): jnp.einsum('kac,kcn->an', sym_amplitudes, sym_integrals, preferred_elemen...  12.8 us
    all_to_all x1, starting transfers between devices, local(): lax.all_to_all(widened, 'row', split_axis=0, concat_axis=1, tiled=True)  12.6 us
  transfers between devices with their start and end apart: 3, of which 3 were waited for; matrix products, arithmetic and copies ran while one was open for 1% of the time, Pallas kernels for 0%

commit v1 on v0

v1 whole, which is shorter than its diff:
```python
import functools

import jax
import jax.numpy as jnp
from jax import lax
from jax.experimental import pallas as pl
from jax.experimental.pallas import tpu as pltpu
from jax.sharding import PartitionSpec as P

NJ = 4
FAR = 2
PARTNERS = (0, 48)
FOLD = 256
QUARTER = FOLD // 4
SEND_TYPE = jnp.float16
SEND_SCALE = 64.0


def colour(row):
    return (row >> 5) & 1


SAME = [row for row in range(64) if colour(row) == 0]


def own_shift():
    mine = colour(lax.axis_index("row"))
    shift = jnp.int32(0)
    for c in range(1, FAR):
        shift = jnp.where(mine == c, PARTNERS[c], shift)
    return shift


def fold_amplitudes(odd, amp_hbm, occ_vec_hbm, occ_hbm, vir_hbm, after_hbm, out_ref, amp_ref, occ_vec_ref, occ_ref, vir_ref, mask_ref, sems):
    cols, rows, occ = amp_ref.shape
    step = cols // (sems.shape[0] - 3)
    small = [
        pltpu.make_async_copy(vir_hbm, vir_ref, sems.at[0]),
        pltpu.make_async_copy(occ_hbm, occ_ref, sems.at[1]),
        pltpu.make_async_copy(occ_vec_hbm, occ_vec_ref, sems.at[2]),
    ]
    large = [
        pltpu.make_async_copy(amp_hbm.at[pl.ds(c, step)], amp_ref.at[pl.ds(c, step)], sems.at[3 + c // step])
        for c in range(0, cols, step)
    ]
    for copy in small + large:
        copy.start()
    for copy in small:
        copy.wait()
    me = lax.axis_index("col")
    first_a = lax.axis_index("row") * rows
    row_id = lax.broadcasted_iota(jnp.int32, (rows, occ), 0)
    a_labels = jnp.zeros((rows, occ), jnp.int32)
    for a in range(rows):
        a_labels = jnp.where(row_id == a, vir_ref[first_a + a], a_labels)
    wanted = occ_ref[0] ^ occ_vec_ref[...] ^ a_labels
    for label in range(8):
        mask_ref[label] = jnp.where(wanted == label, 1.0, 0.0).astype(jnp.bfloat16)
    def run(col, i):
        start = col * cols
        lo, end = i * step, (i + 1) * step
        while lo < end:
            slot = (start + lo) % FOLD
            hi = min(end, lo + QUARTER - slot % QUARTER, FOLD if lo < FOLD else end)
            p = (slot // QUARTER) ^ col
            first = slot % QUARTER
            again = lo >= FOLD
            if p % 2 != odd:
                lo = hi
                continue

            def one(c, lo=lo, p=p, first=first, again=again):
                x = amp_ref[c] * mask_ref[vir_ref[start + c]]
                place = c - lo + first
                if again:
                    x = x + out_ref[p // 2, place]
                out_ref[p // 2, place] = x

            unit = 10
            whole = (hi - lo) // unit * unit

            def body(n, carry, lo=lo, one=one):
                for u in range(unit):
                    one(lo + n * unit + u)
                return carry

            lax.fori_loop(0, whole // unit, body, 0)
            for c in range(lo + whole, hi):
                one(c)
            lo = hi

    for i, copy in enumerate(large):
        copy.wait()
        for col in range(4):

            @pl.when(me == col)
            def _(col=col, i=i):
                run(col, i)


def turn_amplitudes(a_ref, b_ref, c_ref, out_ref, rows_ref, turned_ref):
    _, slots, rows, occ = a_ref.shape
    total = a_ref[0] + b_ref[0] + c_ref[...]
    rows_ref[...] = total.astype(jnp.float32).reshape(slots * rows, occ)
    half = occ // 2
    to = lax.broadcasted_iota(jnp.int32, (occ, occ), 0)
    frm = lax.broadcasted_iota(jnp.int32, (occ, occ), 1)
    pick = (frm == 2 * (to % half) + to // half).astype(jnp.bfloat16)
    for a in range(rows):
        block = rows_ref[pl.ds(a, slots, stride=rows), :].astype(jnp.bfloat16)
        turned = lax.dot_general(pick, block, (((1,), (1,)), ((), ())), preferred_element_type=jnp.float32)
        turned_ref[pl.ds(a, half, stride=rows), :] = jnp.concatenate([turned[:half], turned[half:]], axis=1)
    shift = own_shift()
    for i, member in enumerate(SAME):
        for d, partner in enumerate(PARTNERS):
            row = (member ^ partner) ^ shift
            out_ref[i, d] = turned_ref[pl.ds(pl.multiple_of(row * rows, rows), rows), :].astype(jnp.bfloat16)


def fold_integrals(int_hbm, occ_hbm, vir_hbm, after_hbm, out_ref, lab_ref, vec_ref, int_ref, occ_ref, vir_ref, small, sems):
    _, v, width = int_ref.shape
    near = [pltpu.make_async_copy(vir_hbm, vir_ref, small.at[0]), pltpu.make_async_copy(occ_hbm, occ_ref, small.at[1])]
    step = v // sems.shape[1]
    copies = [
        [
            pltpu.make_async_copy(int_hbm.at[k, pl.ds(c, step)], int_ref.at[k, pl.ds(c, step)], sems.at[k, c // step])
            for c in range(0, v, step)
        ]
        for k in range(2)
    ]
    for copy in near + copies[0] + copies[1]:
        copy.start()
    for copy in near:
        copy.wait()
    begins = []
    for label in range(1, 8):
        lo, hi = jnp.int32(0), jnp.int32(v)
        for _ in range(v.bit_length()):
            mid = jnp.minimum((lo + hi) // 2, v - 1)
            reached = vir_ref[mid] >= label
            lo, hi = jnp.where(reached, lo, mid + 1), jnp.where(reached, mid, hi)
        begins.append(hi)

    def labels_of(orbital):
        return sum((orbital >= begin).astype(jnp.int32) for begin in begins)

    for c in range(0, v, 80):
        at = lax.broadcasted_iota(jnp.int32, (80, 128), 0) + c
        lab_ref[c : c + 80, :] = labels_of(at).astype(jnp.bfloat16)
    vir_vec = labels_of(lax.broadcasted_iota(jnp.int32, (1, width), 1))
    vec_ref[...] = vir_vec
    for k in range(2):
        label = occ_ref[lax.axis_index("row") * 2 + k] ^ occ_ref[1 + lax.axis_index("col")]
        b_labels = (vir_vec ^ label).astype(jnp.bfloat16)
        for i, copy in enumerate(copies[k]):
            copy.wait()
            for c in range(i * step, (i + 1) * step, 80):
                rows = slice(c, c + 80)
                c_labels = lab_ref[rows, :]
                for n in range(FOLD // 128):
                    total = None
                    for b in range(n * 128, width, FOLD):
                        size = min(128, width - b)
                        x = int_ref[k, rows, b : b + size]
                        x = jnp.where(c_labels[:, :size] == b_labels[:, b : b + size], x, jnp.zeros_like(x))
                        if size < 128:
                            x = jnp.concatenate([x, jnp.zeros((80, 128 - size), x.dtype)], axis=1)
                        total = x if total is None else total + x
                    out_ref[k, rows, n * 128 : (n + 1) * 128] = total
        out_ref[k, v:, :] = jnp.zeros((out_ref.shape[1] - v, FOLD), out_ref.dtype)


def contract(terms, last, *refs):
    quarters, partners = sorted({p for p, _ in terms}), sorted({d for _, d in terms})
    cut = len(quarters) + len(partners)
    t_refs, w_refs = refs[: len(quarters)], refs[len(quarters) : cut]
    lab_ref, vec_ref, occ_ref = refs[cut : cut + 3]
    sum_refs, (out_ref, a_lab_ref) = refs[cut + 3 : -2], refs[-2:]
    near, far, rows, lanes = t_refs[0].shape
    v = vec_ref.shape[1]
    me = lax.axis_index("col")
    own = lax.axis_index("row")
    shift = own_shift()
    for i, member in enumerate(SAME):
        label = lab_ref[pl.ds(pl.multiple_of((member ^ shift) * rows, rows), rows), :]
        a_lab_ref[i * rows : (i + 1) * rows, :] = label
    high = lax.broadcasted_iota(jnp.int32, (1, lanes), 1) >= QUARTER

    def labels_at(c):
        x = vec_ref[:, c : min(c + QUARTER, v)]
        if c + QUARTER > v:
            x = jnp.concatenate([x, jnp.full((1, c + QUARTER - v), 64, jnp.int32)], axis=1)
        return jnp.concatenate([x, x], axis=1)

    for col in range(4):

        @pl.when(me == col)
        def _(col=col):
            total = sum_refs[0][...] if sum_refs else None
            a_labels = a_lab_ref[...]
            blocks = [(p, d, c) for p, d in terms for c in range((col ^ p) * QUARTER, v, FOLD)]
            for n in range(0, len(blocks), 2):
                lhs, w = [], []
                for p, d, c in blocks[n : n + 2]:
                    other = 2 * (own ^ PARTNERS[d])
                    wanted = jnp.where(high, occ_ref[other + 1], occ_ref[other]) ^ occ_ref[0]
                    x = t_refs[quarters.index(p)][:, d].reshape(near * rows, lanes)
                    c_labels = (labels_at(c) ^ wanted).astype(jnp.bfloat16)
                    lhs.append(jnp.where(a_labels == c_labels, x, jnp.zeros_like(x)))
                    w += [w_refs[partners.index(d)][k, c : c + QUARTER, :] for k in range(2)]
                lhs = lhs[0] if len(lhs) == 1 else jnp.concatenate(lhs, axis=1)
                part = jnp.dot(lhs, jnp.concatenate(w, axis=0), preferred_element_type=jnp.float32)
                total = part if total is None else total + part
            out_ref[...] = total * SEND_SCALE if last else total


def prepare(res_ref, vir_vec_ref, energy_vec_ref, occ_ref, vir_ref, occ_e_ref, vir_e_ref, plain_ref, factor_ref):
    rows, v = res_ref.shape
    first_a = lax.axis_index("row") * rows
    j = 1 + lax.axis_index("col")
    row_id = lax.broadcasted_iota(jnp.int32, (rows, 128), 0)
    a_labels = jnp.zeros((rows, 128), jnp.int32)
    a_energy = jnp.zeros((rows, 128), jnp.float32)
    for a in range(rows):
        a_labels = jnp.where(row_id == a, vir_ref[first_a + a], a_labels)
        a_energy = jnp.where(row_id == a, vir_e_ref[first_a + a], a_energy)
    b_labels = vir_vec_ref[...] ^ occ_ref[0] ^ occ_ref[j]
    for b in range(0, v, 128):
        width = min(128, v - b)
        at = slice(b, b + width)
        denominator = occ_e_ref[0] - a_energy[:, :width] + (occ_e_ref[j] - energy_vec_ref[:, at])
        plain_ref[:, at] = res_ref[:, at] / denominator
        factor_ref[:, at] = jnp.where(a_labels[:, :width] == b_labels[:, at], (1.0 / SEND_SCALE) / denominator, 0.0)


def finish(part_ref, plain_ref, factor_ref, out_ref):
    total = part_ref[...]
    v = out_ref.shape[1]
    for b in range(0, v, FOLD):
        width = min(FOLD, v - b)
        at = slice(b, b + width)
        out_ref[:, at] = plain_ref[:, at] + factor_ref[:, at] * total[:, :width]


def local(
    amplitudes,
    integrals,
    occupied_irrep,
    virtual_irrep,
    occupied_energy,
    virtual_energy,
    residual_in,
):
    o_win, rows, cols = amplitudes.shape
    occ_local, v, n_local = integrals.shape
    n_row = o_win // occ_local
    near = n_row // FAR
    smem = pl.BlockSpec(memory_space=pltpu.SMEM)
    vmem = pl.BlockSpec(memory_space=pltpu.VMEM)
    hbm = pl.BlockSpec(memory_space=pltpu.HBM)
    big = pltpu.CompilerParams(vmem_limit_bytes=24 * 1024 * 1024)
    occ_vec = occupied_irrep.reshape(1, o_win)

    chunks = 6
    def folded(odd, after):
        return pl.pallas_call(
            functools.partial(fold_amplitudes, odd),
            out_shape=jax.ShapeDtypeStruct((2, QUARTER, rows, o_win), jnp.bfloat16),
            in_specs=[hbm] * 5,
            out_specs=vmem,
            scratch_shapes=[
                pltpu.VMEM((cols, rows, o_win), jnp.bfloat16),
                pltpu.VMEM((1, o_win), jnp.int32),
                pltpu.SMEM((o_win,), jnp.int32),
                pltpu.SMEM((v,), jnp.int32),
                pltpu.VMEM((8, rows, o_win), jnp.bfloat16),
                pltpu.SemaphoreType.DMA((3 + chunks,)),
            ],
            compiler_params=big,
            name="fold_amplitudes",
        )(
            pltpu.with_memory_space_constraint(amplitudes.transpose(2, 1, 0), pltpu.HBM),
            pltpu.with_memory_space_constraint(occ_vec, pltpu.HBM),
            pltpu.with_memory_space_constraint(occupied_irrep, pltpu.HBM),
            pltpu.with_memory_space_constraint(virtual_irrep, pltpu.HBM),
            after,
        )

    send = folded(1, pltpu.with_memory_space_constraint(occupied_irrep, pltpu.HBM))
    keep = folded(0, send)

    def swap(x, p):
        return lax.ppermute(x, "col", [(m, m ^ p) for m in range(4)])

    got = swap(send, 1)
    passed = keep[1] + got[1]
    w, labels, vir_vec = pl.pallas_call(
        fold_integrals,
        out_shape=[
            jax.ShapeDtypeStruct((occ_local, -(-v // QUARTER) * QUARTER, FOLD), jnp.bfloat16),
            jax.ShapeDtypeStruct((v, 128), jnp.bfloat16),
            jax.ShapeDtypeStruct((1, v), jnp.int32),
        ],
        in_specs=[hbm] * 4,
        out_specs=[vmem] * 3,
        scratch_shapes=[
            pltpu.VMEM((occ_local, v, n_local), jnp.bfloat16),
            pltpu.SMEM((o_win,), jnp.int32),
            pltpu.SMEM((v,), jnp.int32),
            pltpu.SemaphoreType.DMA((2,)),
            pltpu.SemaphoreType.DMA((occ_local, 5)),
        ],
        compiler_params=big,
        name="fold_integrals",
    )(
        pltpu.with_memory_space_constraint(integrals, pltpu.HBM),
        pltpu.with_memory_space_constraint(occupied_irrep, pltpu.HBM),
        pltpu.with_memory_space_constraint(virtual_irrep, pltpu.HBM),
        passed,
    )
    far = swap(passed, 2)
    turned = pl.pallas_call(
        turn_amplitudes,
        out_shape=jax.ShapeDtypeStruct((near, FAR, rows, occ_local * QUARTER), jnp.bfloat16),
        in_specs=[vmem] * 3,
        out_specs=vmem,
        scratch_shapes=[
            pltpu.VMEM((QUARTER * rows, o_win), jnp.float32),
            pltpu.VMEM((n_row * rows, o_win), jnp.float32),
        ],
        compiler_params=big,
        cost_estimate=pl.CostEstimate(flops=4 * 10**10, bytes_accessed=10**6, transcendentals=0),
        name="turn_amplitudes",
    )(keep, got, far)
    classes = [[member ^ partner for member in SAME] for partner in PARTNERS]
    mine = lax.all_to_all(turned, "row", split_axis=0, concat_axis=0, tiled=True, axis_index_groups=classes)
    across = swap(mine, 2)

    gathered = [w, lax.ppermute(w, "row", [(r, r ^ PARTNERS[1]) for r in range(n_row)])]
    quarters = [mine, swap(mine, 1), across, swap(across, 1)]

    def contracted(terms, last, sums):
        used = [quarters[p] for p in sorted({p for p, _ in terms})] + [gathered[d] for d in sorted({d for _, d in terms})]
        return pl.pallas_call(
            functools.partial(contract, terms, last),
            out_shape=jax.ShapeDtypeStruct((near * rows, FOLD), jnp.float32),
            in_specs=[vmem] * (len(used) + 2) + [smem] + [vmem] * len(sums),
            out_specs=vmem,
            scratch_shapes=[pltpu.VMEM((near * rows, occ_local * QUARTER), jnp.bfloat16)],
            compiler_params=big,
            name="contract",
        )(*used, labels, vir_vec, occupied_irrep, *sums)

    early = [(0, 0), (1, 0), (2, 0)]
    partial = contracted(early, False, [])
    partial = contracted([(0, 1), (1, 1), (2, 1), (3, 0), (3, 1)], True, [partial])
    parts = lax.all_to_all(
        partial.astype(SEND_TYPE).reshape(near, rows, FOLD),
        "row",
        split_axis=0,
        concat_axis=0,
        tiled=True,
        axis_index_groups=classes,
    )
    plain, factor = pl.pallas_call(
        prepare,
        out_shape=[jax.ShapeDtypeStruct(residual_in.shape, jnp.float32)] * 2,
        in_specs=[vmem] * 3 + [smem] * 4,
        out_specs=[vmem, vmem],
        compiler_params=big,
        name="prepare",
    )(
        residual_in,
        vir_vec,
        virtual_energy.reshape(1, v),
        occupied_irrep,
        virtual_irrep,
        occupied_energy,
        virtual_energy,
    )
    return pl.pallas_call(
        finish,
        out_shape=jax.ShapeDtypeStruct(residual_in.shape, jnp.float32),
        in_specs=[vmem] * 3,
        out_specs=vmem,
        compiler_params=big,
        name="finish",
    )(jnp.sum(parts.astype(jnp.float32), axis=0), plain, factor)


def solution(mesh):
    in_specs = (P(None, "row", "col"), P("row", None, "col"), P(), P(), P(), P(), P("row", "col"))
    out_specs = P("row", "col")
    return jax.shard_map(local, mesh=mesh, in_specs=in_specs, out_specs=out_specs, check_vma=False)
```

time: 542 us -> 65.5 us (0.12)
  waiting for transfers between devices: 484 us -> 21.8 us
  blocking collectives: 0 us -> 21.4 us
  local copies, waits for them, and re-layouts: 14.6 us -> 0.04 us
  between operations: 13.5 us -> 0.17 us
  matrix products: 12.8 us -> 0 us
  Pallas kernels: 0 us -> 11.4 us
    reduce_scatter x1 -> x0, waiting for transfers between devices: 320 us -> none  [local(): lax.psum_scatter(jnp.einsum('kac,kcn->an', sym_amplitudes, sym_integrals,...]
    all_to_all x1, waiting for transfers between devices: 116 us -> 11 us  [local(): lax.all_to_all(partial.astype(SEND_TYPE).reshape(near, rows, FOLD), 'row'...]
    all_gather x1 -> x0, waiting for transfers between devices: 47.4 us -> none  [local(): widened = lax.all_gather(amplitudes, 'col', axis=2, tiled=True)]
    all_to_all x0 -> x1, blocking collectives: none -> 21.4 us  [local(): lax.all_to_all(turned, 'row', split_axis=0, concat_axis=0, tiled=True, ax...]
    dot_general x1 -> x0, matrix products: 12.8 us -> none  [local(): jnp.einsum('kac,kcn->an', sym_amplitudes, sym_integrals, preferred_elemen...]
    pallas_call x0 -> x8, Pallas kernels: none -> 11.4 us  [the longest x1 3.2 us: local(): pl.pallas_call(fold_integrals, out_shape=[jax.ShapeDtypeStruct((occ_local...]
    ppermute x0 -> x6, waiting for transfers between devices: none -> 10.8 us  [the longest x5 10.8 us: swap(): return lax.ppermute(x, 'col', [(m, m ^ p) for m in range(4)])]
    all_gather x1 -> x0, local copies, waits for them, and re-layouts: 9.42 us -> none  [local(): widened = lax.all_gather(amplitudes, 'col', axis=2, tiled=True)]
  transfers between devices with their start and end apart: 3 -> 7, of which waited for: 3 -> 5; matrix products, arithmetic and copies ran while one was open for 1% -> 0% of each run, Pallas kernels for 0% -> 11%
where the time goes in v1:
time: 65.5 us; the launch traced here: 65 us
  waiting for transfers between devices  21.8 us (33%)
  blocking collectives  21.4 us (33%)
  Pallas kernels  11.4 us (17%)
  starting transfers between devices  9.33 us (14%)
  other arithmetic  0.82 us (1%)
    all_to_all x1, blocking collectives, local(): lax.all_to_all(turned, 'row', split_axis=0, concat_axis=0, tiled=True, ax...  21.4 us
    all_to_all x1, waiting for transfers between devices, local(): lax.all_to_all(partial.astype(SEND_TYPE).reshape(near, rows, FOLD), 'row'...  11 us
    ppermute x5, waiting for transfers between devices, swap(): return lax.ppermute(x, 'col', [(m, m ^ p) for m in range(4)])  10.8 us
    all_to_all x1, starting transfers between devices, local(): lax.all_to_all(partial.astype(SEND_TYPE).reshape(near, rows, FOLD), 'row'...  4.81 us
    pallas_call x1, Pallas kernels, local(): pl.pallas_call(fold_integrals, out_shape=[jax.ShapeDtypeStruct((occ_local...  3.2 us
    ppermute x5, starting transfers between devices, swap(): return lax.ppermute(x, 'col', [(m, m ^ p) for m in range(4)])  3.16 us
    pallas_call x2, Pallas kernels, contracted(): pl.pallas_call(functools.partial(contract, terms, last), out_shape=jax.Sh...  3.14 us
    pallas_call x2, Pallas kernels, folded(): pl.pallas_call(functools.partial(fold_amplitudes, odd), out_shape=jax.Sha...  3.02 us
  transfers between devices with their start and end apart: 7, of which 5 were waited for; matrix products, arithmetic and copies ran while one was open for 0% of the time, Pallas kernels for 11%

profile of v1, /device:TPU:4, one launch (start us, length us, event | category | flops | bytes accessed | tf_op | source)
XLA Modules:
  0.0 65.0 jit_solution(5310174673371338134)
XLA Ops:
  0.0 1.5 %fold_amplitudes.2.after_hbm = bf16[2,64,16,128]{3,2,1,0:T(8,128)(2,1)S(1)} custom-call(bf16[300,16,128]{2,1,0:T(8,128)(2,1)} %bitcast.7, s32[1,128]{1,0:T(1,128)} %bitcast.5, s32[128]{0:T(128)} %occ_ref.1, s32[1200]{0:T(1024)} %vir_ref.1, s32[128]{0:T(128)} %occ_ref.1), custom_call_target="tpu_custom_call" | custom-call | tf_op jit(solution)/shard_map/fold_amplitudes/pallas_call | solution.py:266
  1.5 0.1 collective-permute-start
  1.6 1.5 %fold_amplitudes.3.a_ref = bf16[2,64,16,128]{3,2,1,0:T(8,128)(2,1)S(1)} custom-call(bf16[300,16,128]{2,1,0:T(8,128)(2,1)} %bitcast.8, s32[1,128]{1,0:T(1,128)} %bitcast.6, s32[128]{0:T(128)} %occ_ref.1, s32[1200]{0:T(1024)} %vir_ref.1, bf16[2,64,16,128]{3,2,1,0:T(8,128)(2,1)S(1)} %fold_amplitudes.2.after_hbm), custom_call_target="tpu_custom_call" | custom-call | tf_op jit(solution)/shard_map/fold_amplitudes/pallas_call | solution.py:266
  3.1 0.4 collective-permute-done.b_ref
  3.6 2.3 %collective-permute-start.1 = (bf16[64,16,128]{2,1,0:T(8,128)(2,1)S(1)}, bf16[64,16,128]{2,1,0:T(8,128)(2,1)S(1)}, u32[]{:S(2)}, u32[]{:S(2)}) collective-permute-start(bf16[64,16,128]{2,1,0:T(8,128)(2,1)S(1)} %fusion.after_hbm), channel_id=1, source_target_pairs={{0,2},{1,3},{2,0},{3,1},{4,6},{5,7},{6,4},{7,5},{8,10},{9,11},{10,... | collective-permute-start | bytes 786440 | tf_op jit(solution)/shard_map/ppermute | solution.py:293
  5.9 3.2 %fold_integrals.1 = (bf16[2,1216,256]{2,1,0:T(8,128)(2,1)S(1)}, bf16[1200,128]{1,0:T(8,128)(2,1)S(1)}, s32[1,1200]{1,0:T(1,128)S(1)}) custom-call(bf16[2,1200,1200]{2,1,0:T(8,128)(2,1)} %int_hbm.1, s32[128]{0:T(128)} %occ_ref.1, s32[1200]{0:T(1024)} %vir_ref.1, bf16[64,16,128]{2,1,0:T(8,128)(2,1)S(1)} %fusion.after_hbm), custom_call_target="tpu_custom_call" | custom-call | tf_op jit(solution)/shard_map/fold_integrals/pallas_call | solution.py:297
  9.1 0.0 copy-start.2
  9.1 1.4 %collective-permute-start.5 = (bf16[2,1216,256]{2,1,0:T(8,128)(2,1)S(1)}, bf16[2,1216,256]{2,1,0:T(8,128)(2,1)S(1)}, u32[]{:S(2)}, u32[]{:S(2)}) collective-permute-start(bf16[2,1216,256]{2,1,0:T(8,128)(2,1)S(1)} %get-tuple-element.10.refs_3_.refs_4_), channel_id=1, source_target_pairs={{0,192},{4,196},{8,200},{12,204},{16,208},{20,212},{24,216},{28,22... | collective-permute-start | bytes 3735560 | tf_op jit(solution)/shard_map/ppermute | solution.py:339
  10.5 3.1 %collective-permute-done.1.c_ref = bf16[64,16,128]{2,1,0:T(8,128)(2,1)S(1)} collective-permute-done((bf16[64,16,128]{2,1,0:T(8,128)(2,1)S(1)}, bf16[64,16,128]{2,1,0:T(8,128)(2,1)S(1)}, u32[]{:S(2)}, u32[]{:S(2)}) %collective-permute-start.1) | collective-permute-done | bytes 262176 | tf_op jit(solution)/shard_map/ppermute | solution.py:293
  13.5 0.6 turn_amplitudes.1
  14.1 21.4 %all_to_all.10.refs_0_ = bf16[32,2,16,128]{3,2,1,0:T(8,128)(2,1)S(1)} all-to-all(bf16[32,2,16,128]{3,2,1,0:T(8,128)(2,1)S(1)} %turn_amplitudes.1), channel_id=1, replica_groups={{0,4,8,12,16,20,24,28,32,36,40,44,48,52,56,60,64,68,72,76,80,84,88,92,9..., dimensions={0} | all-to-all | bytes 524288 | tf_op jit(solution)/shard_map/all_to_all | solution.py:336
  35.6 0.8 %collective-permute-start.3 = (bf16[32,2,16,128]{3,2,1,0:T(8,128)(2,1)S(1)}, bf16[32,2,16,128]{3,2,1,0:T(8,128)(2,1)S(1)}, u32[]{:S(2)}, u32[]{:S(2)}) collective-permute-start(bf16[32,2,16,128]{3,2,1,0:T(8,128)(2,1)S(1)} %all_to_all.10.refs_0_), channel_id=1, source_target_pairs={{0,2},{1,3},{2,0},{3,1},{4,6},{5,7},{6,4},{7,5},{8,10},{9,11},{10,... | collective-permute-start | bytes 786440 | tf_op jit(solution)/shard_map/ppermute | solution.py:293
  36.3 0.0 collective-permute-start.2
  36.3 7.1 %collective-permute-done.3.refs_2_ = bf16[32,2,16,128]{3,2,1,0:T(8,128)(2,1)S(1)} collective-permute-done((bf16[32,2,16,128]{3,2,1,0:T(8,128)(2,1)S(1)}, bf16[32,2,16,128]{3,2,1,0:T(8,128)(2,1)S(1)}, u32[]{:S(2)}, u32[]{:S(2)}) %collective-permute-start.3) | collective-permute-done | bytes 262176 | tf_op jit(solution)/shard_map/ppermute | solution.py:293
  43.4 0.0 collective-permute-start.4
  43.4 0.0 collective-permute-done.2.refs_1_
  43.4 0.0 copy-done.2
  43.4 1.3 %contract.2.refs_9_ = f32[512,256]{1,0:T(8,128)S(1)} custom-call(bf16[32,2,16,128]{3,2,1,0:T(8,128)(2,1)S(1)} %all_to_all.10.refs_0_, bf16[32,2,16,128]{3,2,1,0:T(8,128)(2,1)S(1)} %collective-permute-done.2.refs_1_, bf16[32,2,16,128]{3,2,1,0:T(8,128)(2,1)S(1)} %collective-permute-done.3.refs_2_, bf16[2,1216,256]{2,1,0:T(8,128)(2,1)S(1)} %get-tuple-element.10.refs_3_.refs_4_, ...), custom_call_target="tpu_custom_call" | custom-call | tf_op jit(solution)/shard_map/contract/pallas_call | solution.py:344
  44.8 0.0 collective-permute-done.5.refs_5_
  44.8 0.2 collective-permute-done.4.refs_3_
  45.0 1.8 %contract.3 = f32[512,256]{1,0:T(8,128)S(1)} custom-call(bf16[32,2,16,128]{3,2,1,0:T(8,128)(2,1)S(1)} %all_to_all.10.refs_0_, bf16[32,2,16,128]{3,2,1,0:T(8,128)(2,1)S(1)} %collective-permute-done.2.refs_1_, bf16[32,2,16,128]{3,2,1,0:T(8,128)(2,1)S(1)} %collective-permute-done.3.refs_2_, bf16[32,2,16,128]{3,2,1,0:T(8,128)(2,1)S(1)} %collective-permute-done.4.refs_3_, ...), custom_call_target="tpu_custom_call" | custom-call | tf_op jit(solution)/shard_map/contract/pallas_call | solution.py:344
  46.8 0.0 copy-start.3
  46.8 0.0 copy-start
  46.8 0.0 copy-start.1
  46.8 0.0 copy-start.4
  46.8 0.7 %convert_element_type.6 = f16[512,256]{1,0:T(8,128)(2,1)} convert(f32[512,256]{1,0:T(8,128)S(1)} %contract.3) | non-fusion elementwise | flops 131072 | bytes 786432 | tf_op jit(solution)/shard_map/convert_element_type | solution.py:358
  47.6 4.8 %all-to-all-start.1 = ((f16[32,16,256]{2,1,0:T(8,128)(2,1)}), f16[32,16,256]{2,1,0:T(8,128)(2,1)S(1)}, u32[]{:S(2)}, u32[]{:S(2)}) async-start(f16[32,16,256]{2,1,0:T(8,128)(2,1)} %bitcast.3), calls=%async_computation.1 | async-start | bytes 524288 | tf_op jit(solution)/shard_map/all_to_all | solution.py:357
  52.4 0.0 copy-done.3
  52.4 0.0 copy-done
  52.5 0.8 %prepare.1 = (f32[16,1200]{1,0:T(8,128)S(1)}, f32[16,1200]{1,0:T(8,128)S(1)}) custom-call(f32[16,1200]{1,0:T(8,128)S(1)} %copy-done.1, s32[1,1200]{1,0:T(1,128)S(1)} %get-tuple-element.12.refs_5_.refs_7_.vir_vec_ref, f32[1,1200]{1,0:T(1,128)S(1)} %reshape.12.energy_vec_ref, s32[128]{0:T(128)S(1)} %copy-done.2, s32[1200]{0:T(1024)S(1)} %copy-done, ...), custom_call_target="tpu_custom_call" | custom-call | tf_op jit(solution)/shard_map/prepare/pallas_call | solution.py:365
  53.2 11.0 %all-to-all-done.1 = f16[32,16,256]{2,1,0:T(8,128)(2,1)S(1)} async-done(((f16[32,16,256]{2,1,0:T(8,128)(2,1)}), f16[32,16,256]{2,1,0:T(8,128)(2,1)S(1)}, u32[]{:S(2)}, u32[]{:S(2)}) %all-to-all-start.1) | async-done | bytes 262176 | tf_op jit(solution)/shard_map/all_to_all | solution.py:357
  64.3 0.6 finish.1
  (5 shorter events, 0.1 us)
Async XLA Ops:
  1.5 2.0 %collective-permute-start = (bf16[2,64,16,128]{3,2,1,0:T(8,128)(2,1)S(1)}, bf16[2,64,16,128]{3,2,1,0:T(8,128)(2,1)S(1)}, u32[]{:S(2)}, u32[]{:S(2)}) collective-permute-start(bf16[2,64,16,128]{3,2,1,0:T(8,128)(2,1)S(1)} %fold_amplitudes.2.after_hbm), channel_id=1, source_target_pairs={{0,1},{1,0},{2,3},{3,2},{4,5},{5,4},{6,7},{7,6},{8,9},{9,8},{10,11... | collective-permute-start | bytes 1572872 | tf_op jit(solution)/shard_map/ppermute | solution.py:293
  3.6 9.9 %collective-permute-start.1 = (bf16[64,16,128]{2,1,0:T(8,128)(2,1)S(1)}, bf16[64,16,128]{2,1,0:T(8,128)(2,1)S(1)}, u32[]{:S(2)}, u32[]{:S(2)}) collective-permute-start(bf16[64,16,128]{2,1,0:T(8,128)(2,1)S(1)} %fusion.after_hbm), channel_id=1, source_target_pairs={{0,2},{1,3},{2,0},{3,1},{4,6},{5,7},{6,4},{7,5},{8,10},{9,11},{10,... | collective-permute-start | bytes 786440 | tf_op jit(solution)/shard_map/ppermute | solution.py:293
  9.1 34.4 %copy-start.2 = (s32[128]{0:T(128)S(1)}, s32[128]{0:T(128)}, u32[]{:S(2)}) copy-start(s32[128]{0:T(128)} %occ_ref.1) | copy-start | bytes 1540
  9.1 35.7 %collective-permute-start.5 = (bf16[2,1216,256]{2,1,0:T(8,128)(2,1)S(1)}, bf16[2,1216,256]{2,1,0:T(8,128)(2,1)S(1)}, u32[]{:S(2)}, u32[]{:S(2)}) collective-permute-start(bf16[2,1216,256]{2,1,0:T(8,128)(2,1)S(1)} %get-tuple-element.10.refs_3_.refs_4_), channel_id=1, source_target_pairs={{0,192},{4,196},{8,200},{12,204},{16,208},{20,212},{24,216},{28,22... | collective-permute-start | bytes 3735560 | tf_op jit(solution)/shard_map/ppermute | solution.py:339
  35.6 7.9 %collective-permute-start.3 = (bf16[32,2,16,128]{3,2,1,0:T(8,128)(2,1)S(1)}, bf16[32,2,16,128]{3,2,1,0:T(8,128)(2,1)S(1)}, u32[]{:S(2)}, u32[]{:S(2)}) collective-permute-start(bf16[32,2,16,128]{3,2,1,0:T(8,128)(2,1)S(1)} %all_to_all.10.refs_0_), channel_id=1, source_target_pairs={{0,2},{1,3},{2,0},{3,1},{4,6},{5,7},{6,4},{7,5},{8,10},{9,11},{10,... | collective-permute-start | bytes 786440 | tf_op jit(solution)/shard_map/ppermute | solution.py:293
  36.3 7.1 %collective-permute-start.2 = (bf16[32,2,16,128]{3,2,1,0:T(8,128)(2,1)S(1)}, bf16[32,2,16,128]{3,2,1,0:T(8,128)(2,1)S(1)}, u32[]{:S(2)}, u32[]{:S(2)}) collective-permute-start(bf16[32,2,16,128]{3,2,1,0:T(8,128)(2,1)S(1)} %all_to_all.10.refs_0_), channel_id=1, source_target_pairs={{0,1},{1,0},{2,3},{3,2},{4,5},{5,4},{6,7},{7,6},{8,9},{9,8},{10,11... | collective-permute-start | bytes 786440 | tf_op jit(solution)/shard_map/ppermute | solution.py:293
  43.4 1.5 %collective-permute-start.4 = (bf16[32,2,16,128]{3,2,1,0:T(8,128)(2,1)S(1)}, bf16[32,2,16,128]{3,2,1,0:T(8,128)(2,1)S(1)}, u32[]{:S(2)}, u32[]{:S(2)}) collective-permute-start(bf16[32,2,16,128]{3,2,1,0:T(8,128)(2,1)S(1)} %collective-permute-done.3.refs_2_), channel_id=1, source_target_pairs={{0,1},{1,0},{2,3},{3,2},{4,5},{5,4},{6,7},{7,6},{8,9},{9,8},{10,11... | collective-permute-start | bytes 786440 | tf_op jit(solution)/shard_map/ppermute | solution.py:293
  46.8 5.6 %copy-start.3 = (f32[1200]{0:T(1024)S(1)}, f32[1200]{0:T(1024)}, u32[]{:S(2)}) copy-start(f32[1200]{0:T(1024)} %vir_e_ref.1) | copy-start | bytes 14404
  46.8 5.6 %copy-start = (s32[1200]{0:T(1024)S(1)}, s32[1200]{0:T(1024)}, u32[]{:S(2)}) copy-start(s32[1200]{0:T(1024)} %vir_ref.1) | copy-start | bytes 14404
  46.8 5.6 %copy-start.1 = (f32[16,1200]{1,0:T(8,128)S(1)}, f32[16,1200]{1,0:T(8,128)}, u32[]{:S(2)}) copy-start(f32[16,1200]{1,0:T(8,128)} %res_ref.1) | copy-start | bytes 230404
  46.8 5.6 %copy-start.4 = (f32[128]{0:T(128)S(1)}, f32[128]{0:T(128)}, u32[]{:S(2)}) copy-start(f32[128]{0:T(128)} %occ_e_ref.1) | copy-start | bytes 1540
  47.6 16.7 %all-to-all-start.1 = ((f16[32,16,256]{2,1,0:T(8,128)(2,1)}), f16[32,16,256]{2,1,0:T(8,128)(2,1)S(1)}, u32[]{:S(2)}, u32[]{:S(2)}) async-start(f16[32,16,256]{2,1,0:T(8,128)(2,1)} %bitcast.3), calls=%async_computation.1 | async-start | bytes 524288 | tf_op jit(solution)/shard_map/all_to_all | solution.py:357

commit v2 on v1

--- a/solution.py
+++ b/solution.py
@@ -20,7 +20,7 @@
     return (row >> 5) & 1
 
 
-SAME = [row for row in range(64) if colour(row) == 0]
+SAME = sorted((row for row in range(64) if colour(row) == 0), key=lambda row: (row & 7, row >> 3))
 
 
 def own_shift():

time: 65.5 us -> 67 us (1.023)
  waiting for transfers between devices: 21.8 us -> 23.2 us
  blocking collectives: 21.4 us -> 22.4 us
    all_to_all x1, waiting for transfers between devices: 11 us -> 12.4 us  [local(): lax.all_to_all(partial.astype(SEND_TYPE).reshape(near, rows, FOLD), 'row'...]
    all_to_all x1, blocking collectives: 21.4 us -> 22.4 us  [local(): lax.all_to_all(turned, 'row', split_axis=0, concat_axis=0, tiled=True, ax...]
where the time goes in v2:
time: 67 us; the launch traced here: 66.7 us
  waiting for transfers between devices  23.2 us (35%)
  blocking collectives  22.4 us (33%)
  Pallas kernels  11.4 us (17%)
  starting transfers between devices  8.75 us (13%)
  other arithmetic  0.82 us (1%)
    all_to_all x1, blocking collectives, local(): lax.all_to_all(turned, 'row', split_axis=0, concat_axis=0, tiled=True, ax...  22.4 us
    all_to_all x1, waiting for transfers between devices, local(): lax.all_to_all(partial.astype(SEND_TYPE).reshape(near, rows, FOLD), 'row'...  12.4 us
    ppermute x5, waiting for transfers between devices, swap(): return lax.ppermute(x, 'col', [(m, m ^ p) for m in range(4)])  10.8 us
    all_to_all x1, starting transfers between devices, local(): lax.all_to_all(partial.astype(SEND_TYPE).reshape(near, rows, FOLD), 'row'...  4.23 us
    pallas_call x1, Pallas kernels, local(): pl.pallas_call(fold_integrals, out_shape=[jax.ShapeDtypeStruct((occ_local...  3.2 us
    ppermute x5, starting transfers between devices, swap(): return lax.ppermute(x, 'col', [(m, m ^ p) for m in range(4)])  3.16 us
    pallas_call x2, Pallas kernels, contracted(): pl.pallas_call(functools.partial(contract, terms, last), out_shape=jax.Sh...  3.15 us
    pallas_call x2, Pallas kernels, folded(): pl.pallas_call(functools.partial(fold_amplitudes, odd), out_shape=jax.Sha...  3.02 us
  transfers between devices with their start and end apart: 7, of which 5 were waited for; matrix products, arithmetic and copies ran while one was open for 0% of the time, Pallas kernels for 11%

profile of v2, /device:TPU:4, one launch (start us, length us, event | category | flops | bytes accessed | tf_op | source)
XLA Modules:
  0.0 66.7 jit_solution(18420462430919412121)
XLA Ops:
  0.0 1.5 %fold_amplitudes.2.after_hbm = bf16[2,64,16,128]{3,2,1,0:T(8,128)(2,1)S(1)} custom-call(bf16[300,16,128]{2,1,0:T(8,128)(2,1)} %bitcast.7, s32[1,128]{1,0:T(1,128)} %bitcast.5, s32[128]{0:T(128)} %occ_ref.1, s32[1200]{0:T(1024)} %vir_ref.1, s32[128]{0:T(128)} %occ_ref.1), custom_call_target="tpu_custom_call" | custom-call | tf_op jit(solution)/shard_map/fold_amplitudes/pallas_call | solution.py:266
  1.5 0.1 collective-permute-start
  1.6 1.5 %fold_amplitudes.3.a_ref = bf16[2,64,16,128]{3,2,1,0:T(8,128)(2,1)S(1)} custom-call(bf16[300,16,128]{2,1,0:T(8,128)(2,1)} %bitcast.8, s32[1,128]{1,0:T(1,128)} %bitcast.6, s32[128]{0:T(128)} %occ_ref.1, s32[1200]{0:T(1024)} %vir_ref.1, bf16[2,64,16,128]{3,2,1,0:T(8,128)(2,1)S(1)} %fold_amplitudes.2.after_hbm), custom_call_target="tpu_custom_call" | custom-call | tf_op jit(solution)/shard_map/fold_amplitudes/pallas_call | solution.py:266
  3.1 0.4 collective-permute-done.b_ref
  3.6 2.3 %collective-permute-start.1 = (bf16[64,16,128]{2,1,0:T(8,128)(2,1)S(1)}, bf16[64,16,128]{2,1,0:T(8,128)(2,1)S(1)}, u32[]{:S(2)}, u32[]{:S(2)}) collective-permute-start(bf16[64,16,128]{2,1,0:T(8,128)(2,1)S(1)} %fusion.after_hbm), channel_id=1, source_target_pairs={{0,2},{1,3},{2,0},{3,1},{4,6},{5,7},{6,4},{7,5},{8,10},{9,11},{10,... | collective-permute-start | bytes 786440 | tf_op jit(solution)/shard_map/ppermute | solution.py:293
  5.9 3.2 %fold_integrals.1 = (bf16[2,1216,256]{2,1,0:T(8,128)(2,1)S(1)}, bf16[1200,128]{1,0:T(8,128)(2,1)S(1)}, s32[1,1200]{1,0:T(1,128)S(1)}) custom-call(bf16[2,1200,1200]{2,1,0:T(8,128)(2,1)} %int_hbm.1, s32[128]{0:T(128)} %occ_ref.1, s32[1200]{0:T(1024)} %vir_ref.1, bf16[64,16,128]{2,1,0:T(8,128)(2,1)S(1)} %fusion.after_hbm), custom_call_target="tpu_custom_call" | custom-call | tf_op jit(solution)/shard_map/fold_integrals/pallas_call | solution.py:297
  9.1 0.0 copy-start.2
  9.1 1.4 %collective-permute-start.5 = (bf16[2,1216,256]{2,1,0:T(8,128)(2,1)S(1)}, bf16[2,1216,256]{2,1,0:T(8,128)(2,1)S(1)}, u32[]{:S(2)}, u32[]{:S(2)}) collective-permute-start(bf16[2,1216,256]{2,1,0:T(8,128)(2,1)S(1)} %get-tuple-element.10.refs_3_.refs_4_), channel_id=1, source_target_pairs={{0,192},{4,196},{8,200},{12,204},{16,208},{20,212},{24,216},{28,22... | collective-permute-start | bytes 3735560 | tf_op jit(solution)/shard_map/ppermute | solution.py:339
  10.5 3.1 %collective-permute-done.1.c_ref = bf16[64,16,128]{2,1,0:T(8,128)(2,1)S(1)} collective-permute-done((bf16[64,16,128]{2,1,0:T(8,128)(2,1)S(1)}, bf16[64,16,128]{2,1,0:T(8,128)(2,1)S(1)}, u32[]{:S(2)}, u32[]{:S(2)}) %collective-permute-start.1) | collective-permute-done | bytes 262176 | tf_op jit(solution)/shard_map/ppermute | solution.py:293
  13.5 0.6 turn_amplitudes.1
  14.1 22.4 %all_to_all.10.refs_0_ = bf16[32,2,16,128]{3,2,1,0:T(8,128)(2,1)S(1)} all-to-all(bf16[32,2,16,128]{3,2,1,0:T(8,128)(2,1)S(1)} %turn_amplitudes.1), channel_id=1, replica_groups={{0,32,64,96,4,36,68,100,8,40,72,104,12,44,76,108,16,48,80,112,20,52,84,..., dimensions={0} | all-to-all | bytes 524288 | tf_op jit(solution)/shard_map/all_to_all | solution.py:336
  36.5 0.8 %collective-permute-start.3 = (bf16[32,2,16,128]{3,2,1,0:T(8,128)(2,1)S(1)}, bf16[32,2,16,128]{3,2,1,0:T(8,128)(2,1)S(1)}, u32[]{:S(2)}, u32[]{:S(2)}) collective-permute-start(bf16[32,2,16,128]{3,2,1,0:T(8,128)(2,1)S(1)} %all_to_all.10.refs_0_), channel_id=1, source_target_pairs={{0,2},{1,3},{2,0},{3,1},{4,6},{5,7},{6,4},{7,5},{8,10},{9,11},{10,... | collective-permute-start | bytes 786440 | tf_op jit(solution)/shard_map/ppermute | solution.py:293
  37.3 0.0 collective-permute-start.2
  37.3 7.1 %collective-permute-done.3.refs_2_ = bf16[32,2,16,128]{3,2,1,0:T(8,128)(2,1)S(1)} collective-permute-done((bf16[32,2,16,128]{3,2,1,0:T(8,128)(2,1)S(1)}, bf16[32,2,16,128]{3,2,1,0:T(8,128)(2,1)S(1)}, u32[]{:S(2)}, u32[]{:S(2)}) %collective-permute-start.3) | collective-permute-done | bytes 262176 | tf_op jit(solution)/shard_map/ppermute | solution.py:293
  44.4 0.0 collective-permute-start.4
  44.4 0.0 collective-permute-done.2.refs_1_
  44.4 0.0 copy-done.2
  44.4 1.3 %contract.2.refs_9_ = f32[512,256]{1,0:T(8,128)S(1)} custom-call(bf16[32,2,16,128]{3,2,1,0:T(8,128)(2,1)S(1)} %all_to_all.10.refs_0_, bf16[32,2,16,128]{3,2,1,0:T(8,128)(2,1)S(1)} %collective-permute-done.2.refs_1_, bf16[32,2,16,128]{3,2,1,0:T(8,128)(2,1)S(1)} %collective-permute-done.3.refs_2_, bf16[2,1216,256]{2,1,0:T(8,128)(2,1)S(1)} %get-tuple-element.10.refs_3_.refs_4_, ...), custom_call_target="tpu_custom_call" | custom-call | tf_op jit(solution)/shard_map/contract/pallas_call | solution.py:344
  45.7 0.0 collective-permute-done.5.refs_5_
  45.7 0.2 collective-permute-done.4.refs_3_
  45.9 1.8 %contract.3 = f32[512,256]{1,0:T(8,128)S(1)} custom-call(bf16[32,2,16,128]{3,2,1,0:T(8,128)(2,1)S(1)} %all_to_all.10.refs_0_, bf16[32,2,16,128]{3,2,1,0:T(8,128)(2,1)S(1)} %collective-permute-done.2.refs_1_, bf16[32,2,16,128]{3,2,1,0:T(8,128)(2,1)S(1)} %collective-permute-done.3.refs_2_, bf16[32,2,16,128]{3,2,1,0:T(8,128)(2,1)S(1)} %collective-permute-done.4.refs_3_, ...), custom_call_target="tpu_custom_call" | custom-call | tf_op jit(solution)/shard_map/contract/pallas_call | solution.py:344
  47.8 0.0 copy-start.3
  47.8 0.0 copy-start
  47.8 0.0 copy-start.1
  47.8 0.0 copy-start.4
  47.8 0.7 %convert_element_type.6 = f16[512,256]{1,0:T(8,128)(2,1)} convert(f32[512,256]{1,0:T(8,128)S(1)} %contract.3) | non-fusion elementwise | flops 131072 | bytes 786432 | tf_op jit(solution)/shard_map/convert_element_type | solution.py:358
  48.6 4.2 %all-to-all-start.1 = ((f16[32,16,256]{2,1,0:T(8,128)(2,1)}), f16[32,16,256]{2,1,0:T(8,128)(2,1)S(1)}, u32[]{:S(2)}, u32[]{:S(2)}) async-start(f16[32,16,256]{2,1,0:T(8,128)(2,1)} %bitcast.3), calls=%async_computation.1 | async-start | bytes 524288 | tf_op jit(solution)/shard_map/all_to_all | solution.py:357
  52.8 0.0 copy-done.3
  52.8 0.0 copy-done
  52.9 0.8 %prepare.1 = (f32[16,1200]{1,0:T(8,128)S(1)}, f32[16,1200]{1,0:T(8,128)S(1)}) custom-call(f32[16,1200]{1,0:T(8,128)S(1)} %copy-done.1, s32[1,1200]{1,0:T(1,128)S(1)} %get-tuple-element.12.refs_5_.refs_7_.vir_vec_ref, f32[1,1200]{1,0:T(1,128)S(1)} %reshape.12.energy_vec_ref, s32[128]{0:T(128)S(1)} %copy-done.2, s32[1200]{0:T(1024)S(1)} %copy-done, ...), custom_call_target="tpu_custom_call" | custom-call | tf_op jit(solution)/shard_map/prepare/pallas_call | solution.py:365
  53.6 12.4 %all-to-all-done.1 = f16[32,16,256]{2,1,0:T(8,128)(2,1)S(1)} async-done(((f16[32,16,256]{2,1,0:T(8,128)(2,1)}), f16[32,16,256]{2,1,0:T(8,128)(2,1)S(1)}, u32[]{:S(2)}, u32[]{:S(2)}) %all-to-all-start.1) | async-done | bytes 262176 | tf_op jit(solution)/shard_map/all_to_all | solution.py:357
  66.1 0.6 finish.1
  (5 shorter events, 0.1 us)
Async XLA Ops:
  1.5 2.0 %collective-permute-start = (bf16[2,64,16,128]{3,2,1,0:T(8,128)(2,1)S(1)}, bf16[2,64,16,128]{3,2,1,0:T(8,128)(2,1)S(1)}, u32[]{:S(2)}, u32[]{:S(2)}) collective-permute-start(bf16[2,64,16,128]{3,2,1,0:T(8,128)(2,1)S(1)} %fold_amplitudes.2.after_hbm), channel_id=1, source_target_pairs={{0,1},{1,0},{2,3},{3,2},{4,5},{5,4},{6,7},{7,6},{8,9},{9,8},{10,11... | collective-permute-start | bytes 1572872 | tf_op jit(solution)/shard_map/ppermute | solution.py:293
  3.6 9.9 %collective-permute-start.1 = (bf16[64,16,128]{2,1,0:T(8,128)(2,1)S(1)}, bf16[64,16,128]{2,1,0:T(8,128)(2,1)S(1)}, u32[]{:S(2)}, u32[]{:S(2)}) collective-permute-start(bf16[64,16,128]{2,1,0:T(8,128)(2,1)S(1)} %fusion.after_hbm), channel_id=1, source_target_pairs={{0,2},{1,3},{2,0},{3,1},{4,6},{5,7},{6,4},{7,5},{8,10},{9,11},{10,... | collective-permute-start | bytes 786440 | tf_op jit(solution)/shard_map/ppermute | solution.py:293
  9.1 35.3 %copy-start.2 = (s32[128]{0:T(128)S(1)}, s32[128]{0:T(128)}, u32[]{:S(2)}) copy-start(s32[128]{0:T(128)} %occ_ref.1) | copy-start | bytes 1540
  9.1 36.6 %collective-permute-start.5 = (bf16[2,1216,256]{2,1,0:T(8,128)(2,1)S(1)}, bf16[2,1216,256]{2,1,0:T(8,128)(2,1)S(1)}, u32[]{:S(2)}, u32[]{:S(2)}) collective-permute-start(bf16[2,1216,256]{2,1,0:T(8,128)(2,1)S(1)} %get-tuple-element.10.refs_3_.refs_4_), channel_id=1, source_target_pairs={{0,192},{4,196},{8,200},{12,204},{16,208},{20,212},{24,216},{28,22... | collective-permute-start | bytes 3735560 | tf_op jit(solution)/shard_map/ppermute | solution.py:339
  36.5 7.9 %collective-permute-start.3 = (bf16[32,2,16,128]{3,2,1,0:T(8,128)(2,1)S(1)}, bf16[32,2,16,128]{3,2,1,0:T(8,128)(2,1)S(1)}, u32[]{:S(2)}, u32[]{:S(2)}) collective-permute-start(bf16[32,2,16,128]{3,2,1,0:T(8,128)(2,1)S(1)} %all_to_all.10.refs_0_), channel_id=1, source_target_pairs={{0,2},{1,3},{2,0},{3,1},{4,6},{5,7},{6,4},{7,5},{8,10},{9,11},{10,... | collective-permute-start | bytes 786440 | tf_op jit(solution)/shard_map/ppermute | solution.py:293
  37.3 7.1 %collective-permute-start.2 = (bf16[32,2,16,128]{3,2,1,0:T(8,128)(2,1)S(1)}, bf16[32,2,16,128]{3,2,1,0:T(8,128)(2,1)S(1)}, u32[]{:S(2)}, u32[]{:S(2)}) collective-permute-start(bf16[32,2,16,128]{3,2,1,0:T(8,128)(2,1)S(1)} %all_to_all.10.refs_0_), channel_id=1, source_target_pairs={{0,1},{1,0},{2,3},{3,2},{4,5},{5,4},{6,7},{7,6},{8,9},{9,8},{10,11... | collective-permute-start | bytes 786440 | tf_op jit(solution)/shard_map/ppermute | solution.py:293
  44.4 1.5 %collective-permute-start.4 = (bf16[32,2,16,128]{3,2,1,0:T(8,128)(2,1)S(1)}, bf16[32,2,16,128]{3,2,1,0:T(8,128)(2,1)S(1)}, u32[]{:S(2)}, u32[]{:S(2)}) collective-permute-start(bf16[32,2,16,128]{3,2,1,0:T(8,128)(2,1)S(1)} %collective-permute-done.3.refs_2_), channel_id=1, source_target_pairs={{0,1},{1,0},{2,3},{3,2},{4,5},{5,4},{6,7},{7,6},{8,9},{9,8},{10,11... | collective-permute-start | bytes 786440 | tf_op jit(solution)/shard_map/ppermute | solution.py:293
  47.8 5.0 %copy-start.3 = (f32[1200]{0:T(1024)S(1)}, f32[1200]{0:T(1024)}, u32[]{:S(2)}) copy-start(f32[1200]{0:T(1024)} %vir_e_ref.1) | copy-start | bytes 14404
  47.8 5.0 %copy-start = (s32[1200]{0:T(1024)S(1)}, s32[1200]{0:T(1024)}, u32[]{:S(2)}) copy-start(s32[1200]{0:T(1024)} %vir_ref.1) | copy-start | bytes 14404
  47.8 5.0 %copy-start.1 = (f32[16,1200]{1,0:T(8,128)S(1)}, f32[16,1200]{1,0:T(8,128)}, u32[]{:S(2)}) copy-start(f32[16,1200]{1,0:T(8,128)} %res_ref.1) | copy-start | bytes 230404
  47.8 5.0 %copy-start.4 = (f32[128]{0:T(128)S(1)}, f32[128]{0:T(128)}, u32[]{:S(2)}) copy-start(f32[128]{0:T(128)} %occ_e_ref.1) | copy-start | bytes 1540
  48.6 17.4 %all-to-all-start.1 = ((f16[32,16,256]{2,1,0:T(8,128)(2,1)}), f16[32,16,256]{2,1,0:T(8,128)(2,1)S(1)}, u32[]{:S(2)}, u32[]{:S(2)}) async-start(f16[32,16,256]{2,1,0:T(8,128)(2,1)} %bitcast.3), calls=%async_computation.1 | async-start | bytes 524288 | tf_op jit(solution)/shard_map/all_to_all | solution.py:357

commit v3 on v1

--- a/solution.py
+++ b/solution.py
@@ -11,6 +11,7 @@
 FAR = 2
 PARTNERS = (0, 48)
 FOLD = 256
+GROUP = 4
 QUARTER = FOLD // 4
 SEND_TYPE = jnp.float16
 SEND_SCALE = 64.0
@@ -199,9 +200,9 @@
             total = sum_refs[0][...] if sum_refs else None
             a_labels = a_lab_ref[...]
             blocks = [(p, d, c) for p, d in terms for c in range((col ^ p) * QUARTER, v, FOLD)]
-            for n in range(0, len(blocks), 2):
+            for n in range(0, len(blocks), GROUP):
                 lhs, w = [], []
-                for p, d, c in blocks[n : n + 2]:
+                for p, d, c in blocks[n : n + GROUP]:
                     other = 2 * (own ^ PARTNERS[d])
                     wanted = jnp.where(high, occ_ref[other + 1], occ_ref[other]) ^ occ_ref[0]
                     x = t_refs[quarters.index(p)][:, d].reshape(near * rows, lanes)

time: 65.5 us -> 65.5 us (level)
  no operation moved by 1% of the time
where the time goes in v3:
time: 65.5 us; the launch traced here: 65 us
  waiting for transfers between devices  21.8 us (33%)
  blocking collectives  21.4 us (33%)
  Pallas kernels  11.4 us (17%)
  starting transfers between devices  9.33 us (14%)
  other arithmetic  0.82 us (1%)
    all_to_all x1, blocking collectives, local(): lax.all_to_all(turned, 'row', split_axis=0, concat_axis=0, tiled=True, ax...  21.4 us
    all_to_all x1, waiting for transfers between devices, local(): lax.all_to_all(partial.astype(SEND_TYPE).reshape(near, rows, FOLD), 'row'...  11 us
    ppermute x5, waiting for transfers between devices, swap(): return lax.ppermute(x, 'col', [(m, m ^ p) for m in range(4)])  10.8 us
    all_to_all x1, starting transfers between devices, local(): lax.all_to_all(partial.astype(SEND_TYPE).reshape(near, rows, FOLD), 'row'...  4.81 us
    pallas_call x1, Pallas kernels, local(): pl.pallas_call(fold_integrals, out_shape=[jax.ShapeDtypeStruct((occ_local...  3.2 us
    ppermute x5, starting transfers between devices, swap(): return lax.ppermute(x, 'col', [(m, m ^ p) for m in range(4)])  3.16 us
    pallas_call x2, Pallas kernels, contracted(): pl.pallas_call(functools.partial(contract, terms, last), out_shape=jax.Sh...  3.14 us
    pallas_call x2, Pallas kernels, folded(): pl.pallas_call(functools.partial(fold_amplitudes, odd), out_shape=jax.Sha...  3.02 us
  transfers between devices with their start and end apart: 7, of which 5 were waited for; matrix products, arithmetic and copies ran while one was open for 0% of the time, Pallas kernels for 11%

profile of v3, /device:TPU:4, one launch (start us, length us, event | category | flops | bytes accessed | tf_op | source)
XLA Modules:
  0.0 65.0 jit_solution(16789795041154541231)
XLA Ops:
  0.0 1.5 %fold_amplitudes.2.after_hbm = bf16[2,64,16,128]{3,2,1,0:T(8,128)(2,1)S(1)} custom-call(bf16[300,16,128]{2,1,0:T(8,128)(2,1)} %bitcast.7, s32[1,128]{1,0:T(1,128)} %bitcast.5, s32[128]{0:T(128)} %occ_ref.1, s32[1200]{0:T(1024)} %vir_ref.1, s32[128]{0:T(128)} %occ_ref.1), custom_call_target="tpu_custom_call" | custom-call | tf_op jit(solution)/shard_map/fold_amplitudes/pallas_call | solution.py:267
  1.5 0.1 collective-permute-start
  1.6 1.5 %fold_amplitudes.3.a_ref = bf16[2,64,16,128]{3,2,1,0:T(8,128)(2,1)S(1)} custom-call(bf16[300,16,128]{2,1,0:T(8,128)(2,1)} %bitcast.8, s32[1,128]{1,0:T(1,128)} %bitcast.6, s32[128]{0:T(128)} %occ_ref.1, s32[1200]{0:T(1024)} %vir_ref.1, bf16[2,64,16,128]{3,2,1,0:T(8,128)(2,1)S(1)} %fold_amplitudes.2.after_hbm), custom_call_target="tpu_custom_call" | custom-call | tf_op jit(solution)/shard_map/fold_amplitudes/pallas_call | solution.py:267
  3.1 0.4 collective-permute-done.b_ref
  3.6 2.3 %collective-permute-start.1 = (bf16[64,16,128]{2,1,0:T(8,128)(2,1)S(1)}, bf16[64,16,128]{2,1,0:T(8,128)(2,1)S(1)}, u32[]{:S(2)}, u32[]{:S(2)}) collective-permute-start(bf16[64,16,128]{2,1,0:T(8,128)(2,1)S(1)} %fusion.after_hbm), channel_id=1, source_target_pairs={{0,2},{1,3},{2,0},{3,1},{4,6},{5,7},{6,4},{7,5},{8,10},{9,11},{10,... | collective-permute-start | bytes 786440 | tf_op jit(solution)/shard_map/ppermute | solution.py:294
  5.9 3.2 %fold_integrals.1 = (bf16[2,1216,256]{2,1,0:T(8,128)(2,1)S(1)}, bf16[1200,128]{1,0:T(8,128)(2,1)S(1)}, s32[1,1200]{1,0:T(1,128)S(1)}) custom-call(bf16[2,1200,1200]{2,1,0:T(8,128)(2,1)} %int_hbm.1, s32[128]{0:T(128)} %occ_ref.1, s32[1200]{0:T(1024)} %vir_ref.1, bf16[64,16,128]{2,1,0:T(8,128)(2,1)S(1)} %fusion.after_hbm), custom_call_target="tpu_custom_call" | custom-call | tf_op jit(solution)/shard_map/fold_integrals/pallas_call | solution.py:298
  9.1 0.0 copy-start.2
  9.1 1.4 %collective-permute-start.5 = (bf16[2,1216,256]{2,1,0:T(8,128)(2,1)S(1)}, bf16[2,1216,256]{2,1,0:T(8,128)(2,1)S(1)}, u32[]{:S(2)}, u32[]{:S(2)}) collective-permute-start(bf16[2,1216,256]{2,1,0:T(8,128)(2,1)S(1)} %get-tuple-element.10.refs_3_.refs_4_), channel_id=1, source_target_pairs={{0,192},{4,196},{8,200},{12,204},{16,208},{20,212},{24,216},{28,22... | collective-permute-start | bytes 3735560 | tf_op jit(solution)/shard_map/ppermute | solution.py:340
  10.5 3.1 %collective-permute-done.1.c_ref = bf16[64,16,128]{2,1,0:T(8,128)(2,1)S(1)} collective-permute-done((bf16[64,16,128]{2,1,0:T(8,128)(2,1)S(1)}, bf16[64,16,128]{2,1,0:T(8,128)(2,1)S(1)}, u32[]{:S(2)}, u32[]{:S(2)}) %collective-permute-start.1) | collective-permute-done | bytes 262176 | tf_op jit(solution)/shard_map/ppermute | solution.py:294
  13.5 0.6 turn_amplitudes.1
  14.1 21.4 %all_to_all.10.refs_0_ = bf16[32,2,16,128]{3,2,1,0:T(8,128)(2,1)S(1)} all-to-all(bf16[32,2,16,128]{3,2,1,0:T(8,128)(2,1)S(1)} %turn_amplitudes.1), channel_id=1, replica_groups={{0,4,8,12,16,20,24,28,32,36,40,44,48,52,56,60,64,68,72,76,80,84,88,92,9..., dimensions={0} | all-to-all | bytes 524288 | tf_op jit(solution)/shard_map/all_to_all | solution.py:337
  35.6 0.8 %collective-permute-start.3 = (bf16[32,2,16,128]{3,2,1,0:T(8,128)(2,1)S(1)}, bf16[32,2,16,128]{3,2,1,0:T(8,128)(2,1)S(1)}, u32[]{:S(2)}, u32[]{:S(2)}) collective-permute-start(bf16[32,2,16,128]{3,2,1,0:T(8,128)(2,1)S(1)} %all_to_all.10.refs_0_), channel_id=1, source_target_pairs={{0,2},{1,3},{2,0},{3,1},{4,6},{5,7},{6,4},{7,5},{8,10},{9,11},{10,... | collective-permute-start | bytes 786440 | tf_op jit(solution)/shard_map/ppermute | solution.py:294
  36.3 0.0 collective-permute-start.2
  36.3 7.1 %collective-permute-done.3.refs_2_ = bf16[32,2,16,128]{3,2,1,0:T(8,128)(2,1)S(1)} collective-permute-done((bf16[32,2,16,128]{3,2,1,0:T(8,128)(2,1)S(1)}, bf16[32,2,16,128]{3,2,1,0:T(8,128)(2,1)S(1)}, u32[]{:S(2)}, u32[]{:S(2)}) %collective-permute-start.3) | collective-permute-done | bytes 262176 | tf_op jit(solution)/shard_map/ppermute | solution.py:294
  43.4 0.0 collective-permute-start.4
  43.4 0.0 collective-permute-done.2.refs_1_
  43.4 0.0 copy-done.2
  43.4 1.3 %contract.2.refs_9_ = f32[512,256]{1,0:T(8,128)S(1)} custom-call(bf16[32,2,16,128]{3,2,1,0:T(8,128)(2,1)S(1)} %all_to_all.10.refs_0_, bf16[32,2,16,128]{3,2,1,0:T(8,128)(2,1)S(1)} %collective-permute-done.2.refs_1_, bf16[32,2,16,128]{3,2,1,0:T(8,128)(2,1)S(1)} %collective-permute-done.3.refs_2_, bf16[2,1216,256]{2,1,0:T(8,128)(2,1)S(1)} %get-tuple-element.10.refs_3_.refs_4_, ...), custom_call_target="tpu_custom_call" | custom-call | tf_op jit(solution)/shard_map/contract/pallas_call | solution.py:345
  44.8 0.0 collective-permute-done.5.refs_5_
  44.8 0.2 collective-permute-done.4.refs_3_
  45.0 1.8 %contract.3 = f32[512,256]{1,0:T(8,128)S(1)} custom-call(bf16[32,2,16,128]{3,2,1,0:T(8,128)(2,1)S(1)} %all_to_all.10.refs_0_, bf16[32,2,16,128]{3,2,1,0:T(8,128)(2,1)S(1)} %collective-permute-done.2.refs_1_, bf16[32,2,16,128]{3,2,1,0:T(8,128)(2,1)S(1)} %collective-permute-done.3.refs_2_, bf16[32,2,16,128]{3,2,1,0:T(8,128)(2,1)S(1)} %collective-permute-done.4.refs_3_, ...), custom_call_target="tpu_custom_call" | custom-call | tf_op jit(solution)/shard_map/contract/pallas_call | solution.py:345
  46.8 0.0 copy-start.3
  46.8 0.0 copy-start
  46.8 0.0 copy-start.1
  46.8 0.0 copy-start.4
  46.8 0.7 %convert_element_type.6 = f16[512,256]{1,0:T(8,128)(2,1)} convert(f32[512,256]{1,0:T(8,128)S(1)} %contract.3) | non-fusion elementwise | flops 131072 | bytes 786432 | tf_op jit(solution)/shard_map/convert_element_type | solution.py:359
  47.6 4.8 %all-to-all-start.1 = ((f16[32,16,256]{2,1,0:T(8,128)(2,1)}), f16[32,16,256]{2,1,0:T(8,128)(2,1)S(1)}, u32[]{:S(2)}, u32[]{:S(2)}) async-start(f16[32,16,256]{2,1,0:T(8,128)(2,1)} %bitcast.3), calls=%async_computation.1 | async-start | bytes 524288 | tf_op jit(solution)/shard_map/all_to_all | solution.py:358
  52.4 0.0 copy-done.3
  52.4 0.0 copy-done
  52.5 0.8 %prepare.1 = (f32[16,1200]{1,0:T(8,128)S(1)}, f32[16,1200]{1,0:T(8,128)S(1)}) custom-call(f32[16,1200]{1,0:T(8,128)S(1)} %copy-done.1, s32[1,1200]{1,0:T(1,128)S(1)} %get-tuple-element.12.refs_5_.refs_7_.vir_vec_ref, f32[1,1200]{1,0:T(1,128)S(1)} %reshape.12.energy_vec_ref, s32[128]{0:T(128)S(1)} %copy-done.2, s32[1200]{0:T(1024)S(1)} %copy-done, ...), custom_call_target="tpu_custom_call" | custom-call | tf_op jit(solution)/shard_map/prepare/pallas_call | solution.py:366
  53.2 11.0 %all-to-all-done.1 = f16[32,16,256]{2,1,0:T(8,128)(2,1)S(1)} async-done(((f16[32,16,256]{2,1,0:T(8,128)(2,1)}), f16[32,16,256]{2,1,0:T(8,128)(2,1)S(1)}, u32[]{:S(2)}, u32[]{:S(2)}) %all-to-all-start.1) | async-done | bytes 262176 | tf_op jit(solution)/shard_map/all_to_all | solution.py:358
  64.3 0.6 finish.1
  (5 shorter events, 0.1 us)
Async XLA Ops:
  1.5 2.0 %collective-permute-start = (bf16[2,64,16,128]{3,2,1,0:T(8,128)(2,1)S(1)}, bf16[2,64,16,128]{3,2,1,0:T(8,128)(2,1)S(1)}, u32[]{:S(2)}, u32[]{:S(2)}) collective-permute-start(bf16[2,64,16,128]{3,2,1,0:T(8,128)(2,1)S(1)} %fold_amplitudes.2.after_hbm), channel_id=1, source_target_pairs={{0,1},{1,0},{2,3},{3,2},{4,5},{5,4},{6,7},{7,6},{8,9},{9,8},{10,11... | collective-permute-start | bytes 1572872 | tf_op jit(solution)/shard_map/ppermute | solution.py:294
  3.6 9.9 %collective-permute-start.1 = (bf16[64,16,128]{2,1,0:T(8,128)(2,1)S(1)}, bf16[64,16,128]{2,1,0:T(8,128)(2,1)S(1)}, u32[]{:S(2)}, u32[]{:S(2)}) collective-permute-start(bf16[64,16,128]{2,1,0:T(8,128)(2,1)S(1)} %fusion.after_hbm), channel_id=1, source_target_pairs={{0,2},{1,3},{2,0},{3,1},{4,6},{5,7},{6,4},{7,5},{8,10},{9,11},{10,... | collective-permute-start | bytes 786440 | tf_op jit(solution)/shard_map/ppermute | solution.py:294
  9.1 34.4 %copy-start.2 = (s32[128]{0:T(128)S(1)}, s32[128]{0:T(128)}, u32[]{:S(2)}) copy-start(s32[128]{0:T(128)} %occ_ref.1) | copy-start | bytes 1540
  9.1 35.7 %collective-permute-start.5 = (bf16[2,1216,256]{2,1,0:T(8,128)(2,1)S(1)}, bf16[2,1216,256]{2,1,0:T(8,128)(2,1)S(1)}, u32[]{:S(2)}, u32[]{:S(2)}) collective-permute-start(bf16[2,1216,256]{2,1,0:T(8,128)(2,1)S(1)} %get-tuple-element.10.refs_3_.refs_4_), channel_id=1, source_target_pairs={{0,192},{4,196},{8,200},{12,204},{16,208},{20,212},{24,216},{28,22... | collective-permute-start | bytes 3735560 | tf_op jit(solution)/shard_map/ppermute | solution.py:340
  35.6 7.9 %collective-permute-start.3 = (bf16[32,2,16,128]{3,2,1,0:T(8,128)(2,1)S(1)}, bf16[32,2,16,128]{3,2,1,0:T(8,128)(2,1)S(1)}, u32[]{:S(2)}, u32[]{:S(2)}) collective-permute-start(bf16[32,2,16,128]{3,2,1,0:T(8,128)(2,1)S(1)} %all_to_all.10.refs_0_), channel_id=1, source_target_pairs={{0,2},{1,3},{2,0},{3,1},{4,6},{5,7},{6,4},{7,5},{8,10},{9,11},{10,... | collective-permute-start | bytes 786440 | tf_op jit(solution)/shard_map/ppermute | solution.py:294
  36.3 7.1 %collective-permute-start.2 = (bf16[32,2,16,128]{3,2,1,0:T(8,128)(2,1)S(1)}, bf16[32,2,16,128]{3,2,1,0:T(8,128)(2,1)S(1)}, u32[]{:S(2)}, u32[]{:S(2)}) collective-permute-start(bf16[32,2,16,128]{3,2,1,0:T(8,128)(2,1)S(1)} %all_to_all.10.refs_0_), channel_id=1, source_target_pairs={{0,1},{1,0},{2,3},{3,2},{4,5},{5,4},{6,7},{7,6},{8,9},{9,8},{10,11... | collective-permute-start | bytes 786440 | tf_op jit(solution)/shard_map/ppermute | solution.py:294
  43.4 1.5 %collective-permute-start.4 = (bf16[32,2,16,128]{3,2,1,0:T(8,128)(2,1)S(1)}, bf16[32,2,16,128]{3,2,1,0:T(8,128)(2,1)S(1)}, u32[]{:S(2)}, u32[]{:S(2)}) collective-permute-start(bf16[32,2,16,128]{3,2,1,0:T(8,128)(2,1)S(1)} %collective-permute-done.3.refs_2_), channel_id=1, source_target_pairs={{0,1},{1,0},{2,3},{3,2},{4,5},{5,4},{6,7},{7,6},{8,9},{9,8},{10,11... | collective-permute-start | bytes 786440 | tf_op jit(solution)/shard_map/ppermute | solution.py:294
  46.8 5.6 %copy-start.3 = (f32[1200]{0:T(1024)S(1)}, f32[1200]{0:T(1024)}, u32[]{:S(2)}) copy-start(f32[1200]{0:T(1024)} %vir_e_ref.1) | copy-start | bytes 14404
  46.8 5.6 %copy-start = (s32[1200]{0:T(1024)S(1)}, s32[1200]{0:T(1024)}, u32[]{:S(2)}) copy-start(s32[1200]{0:T(1024)} %vir_ref.1) | copy-start | bytes 14404
  46.8 5.6 %copy-start.1 = (f32[16,1200]{1,0:T(8,128)S(1)}, f32[16,1200]{1,0:T(8,128)}, u32[]{:S(2)}) copy-start(f32[16,1200]{1,0:T(8,128)} %res_ref.1) | copy-start | bytes 230404
  46.8 5.6 %copy-start.4 = (f32[128]{0:T(128)S(1)}, f32[128]{0:T(128)}, u32[]{:S(2)}) copy-start(f32[128]{0:T(128)} %occ_e_ref.1) | copy-start | bytes 1540
  47.6 16.7 %all-to-all-start.1 = ((f16[32,16,256]{2,1,0:T(8,128)(2,1)}), f16[32,16,256]{2,1,0:T(8,128)(2,1)S(1)}, u32[]{:S(2)}, u32[]{:S(2)}) async-start(f16[32,16,256]{2,1,0:T(8,128)(2,1)} %bitcast.3), calls=%async_computation.1 | async-start | bytes 524288 | tf_op jit(solution)/shard_map/all_to_all | solution.py:358

commit v4 on v1

--- a/solution.py
+++ b/solution.py
@@ -117,7 +117,7 @@
             out_ref[i, d] = turned_ref[pl.ds(pl.multiple_of(row * rows, rows), rows), :].astype(jnp.bfloat16)
 
 
-def fold_integrals(int_hbm, occ_hbm, vir_hbm, after_hbm, out_ref, lab_ref, vec_ref, int_ref, occ_ref, vir_ref, small, sems):
+def fold_integrals(int_hbm, occ_hbm, vir_hbm, after_hbm, out_ref, lab_ref, vec_ref, tab_ref, int_ref, occ_ref, vir_ref, small, sems):
     _, v, width = int_ref.shape
     near = [pltpu.make_async_copy(vir_hbm, vir_ref, small.at[0]), pltpu.make_async_copy(occ_hbm, occ_ref, small.at[1])]
     step = v // sems.shape[1]
@@ -149,6 +149,14 @@
         lab_ref[c : c + 80, :] = labels_of(at).astype(jnp.bfloat16)
     vir_vec = labels_of(lax.broadcasted_iota(jnp.int32, (1, width), 1))
     vec_ref[...] = vir_vec
+    for block in range(tab_ref.shape[0]):
+        size = min(QUARTER, v - block * QUARTER)
+        x = jnp.full((1, QUARTER), 64, jnp.int32)
+        if size > 0:
+            x = vir_vec[:, block * QUARTER : block * QUARTER + size]
+            if size < QUARTER:
+                x = jnp.concatenate([x, jnp.full((1, QUARTER - size), 64, jnp.int32)], axis=1)
+        tab_ref[block : block + 1, :] = jnp.concatenate([x, x], axis=1)
     for k in range(2):
         label = occ_ref[lax.axis_index("row") * 2 + k] ^ occ_ref[1 + lax.axis_index("col")]
         b_labels = (vir_vec ^ label).astype(jnp.bfloat16)
@@ -174,10 +182,10 @@
     quarters, partners = sorted({p for p, _ in terms}), sorted({d for _, d in terms})
     cut = len(quarters) + len(partners)
     t_refs, w_refs = refs[: len(quarters)], refs[len(quarters) : cut]
-    lab_ref, vec_ref, occ_ref = refs[cut : cut + 3]
+    lab_ref, tab_ref, occ_ref = refs[cut : cut + 3]
     sum_refs, (out_ref, a_lab_ref) = refs[cut + 3 : -2], refs[-2:]
     near, far, rows, lanes = t_refs[0].shape
-    v = vec_ref.shape[1]
+    tall = w_refs[0].shape[1]
     me = lax.axis_index("col")
     own = lax.axis_index("row")
     shift = own_shift()
@@ -185,33 +193,24 @@
         label = lab_ref[pl.ds(pl.multiple_of((member ^ shift) * rows, rows), rows), :]
         a_lab_ref[i * rows : (i + 1) * rows, :] = label
     high = lax.broadcasted_iota(jnp.int32, (1, lanes), 1) >= QUARTER
-
-    def labels_at(c):
-        x = vec_ref[:, c : min(c + QUARTER, v)]
-        if c + QUARTER > v:
-            x = jnp.concatenate([x, jnp.full((1, c + QUARTER - v), 64, jnp.int32)], axis=1)
-        return jnp.concatenate([x, x], axis=1)
-
-    for col in range(4):
-
-        @pl.when(me == col)
-        def _(col=col):
-            total = sum_refs[0][...] if sum_refs else None
-            a_labels = a_lab_ref[...]
-            blocks = [(p, d, c) for p, d in terms for c in range((col ^ p) * QUARTER, v, FOLD)]
-            for n in range(0, len(blocks), 2):
-                lhs, w = [], []
-                for p, d, c in blocks[n : n + 2]:
-                    other = 2 * (own ^ PARTNERS[d])
-                    wanted = jnp.where(high, occ_ref[other + 1], occ_ref[other]) ^ occ_ref[0]
-                    x = t_refs[quarters.index(p)][:, d].reshape(near * rows, lanes)
-                    c_labels = (labels_at(c) ^ wanted).astype(jnp.bfloat16)
-                    lhs.append(jnp.where(a_labels == c_labels, x, jnp.zeros_like(x)))
-                    w += [w_refs[partners.index(d)][k, c : c + QUARTER, :] for k in range(2)]
-                lhs = lhs[0] if len(lhs) == 1 else jnp.concatenate(lhs, axis=1)
-                part = jnp.dot(lhs, jnp.concatenate(w, axis=0), preferred_element_type=jnp.float32)
-                total = part if total is None else total + part
-            out_ref[...] = total * SEND_SCALE if last else total
+    a_labels = a_lab_ref[...]
+    total = sum_refs[0][...] if sum_refs else None
+    blocks = [(p, d, t) for p, d in terms for t in range(tab_ref.shape[0] // 4)]
+    for n in range(0, len(blocks), 2):
+        lhs, w = [], []
+        for p, d, t in blocks[n : n + 2]:
+            other = 2 * (own ^ PARTNERS[d])
+            wanted = jnp.where(high, occ_ref[other + 1], occ_ref[other]) ^ occ_ref[0]
+            block = 4 * t + (me ^ p)
+            x = t_refs[quarters.index(p)][:, d].reshape(near * rows, lanes)
+            c_labels = (tab_ref[pl.ds(block, 1), :] ^ wanted).astype(jnp.bfloat16)
+            lhs.append(jnp.where(a_labels == c_labels, x, jnp.zeros_like(x)))
+            c = pl.multiple_of(jnp.minimum(block * QUARTER, tall - QUARTER), QUARTER)
+            w += [w_refs[partners.index(d)][k, pl.ds(c, QUARTER), :] for k in range(2)]
+        lhs = lhs[0] if len(lhs) == 1 else jnp.concatenate(lhs, axis=1)
+        part = jnp.dot(lhs, jnp.concatenate(w, axis=0), preferred_element_type=jnp.float32)
+        total = part if total is None else total + part
+    out_ref[...] = total * SEND_SCALE if last else total
 
 
 def prepare(res_ref, vir_vec_ref, energy_vec_ref, occ_ref, vir_ref, occ_e_ref, vir_e_ref, plain_ref, factor_ref):
@@ -294,15 +293,16 @@
 
     got = swap(send, 1)
     passed = keep[1] + got[1]
-    w, labels, vir_vec = pl.pallas_call(
+    w, labels, vir_vec, table = pl.pallas_call(
         fold_integrals,
         out_shape=[
             jax.ShapeDtypeStruct((occ_local, -(-v // QUARTER) * QUARTER, FOLD), jnp.bfloat16),
             jax.ShapeDtypeStruct((v, 128), jnp.bfloat16),
             jax.ShapeDtypeStruct((1, v), jnp.int32),
+            jax.ShapeDtypeStruct((4 * (-(-v // FOLD)), 2 * QUARTER), jnp.int32),
         ],
         in_specs=[hbm] * 4,
-        out_specs=[vmem] * 3,
+        out_specs=[vmem] * 4,
         scratch_shapes=[
             pltpu.VMEM((occ_local, v, n_local), jnp.bfloat16),
             pltpu.SMEM((o_win,), jnp.int32),
@@ -337,7 +337,7 @@
     across = swap(mine, 2)
 
     gathered = [w, lax.ppermute(w, "row", [(r, r ^ PARTNERS[1]) for r in range(n_row)])]
-    quarters = [mine, swap(mine, 1), across, swap(across, 1)]
+    quarters = [mine, swap(mine, 1)]
 
     def contracted(terms, last, sums):
         used = [quarters[p] for p in sorted({p for p, _ in terms})] + [gathered[d] for d in sorted({d for _, d in terms})]
@@ -349,10 +349,12 @@
             scratch_shapes=[pltpu.VMEM((near * rows, occ_local * QUARTER), jnp.bfloat16)],
             compiler_params=big,
             name="contract",
-        )(*used, labels, vir_vec, occupied_irrep, *sums)
-
-    early = [(0, 0), (1, 0), (2, 0)]
-    partial = contracted(early, False, [])
+        )(*used, labels, table, occupied_irrep, *sums)
+
+    partial = contracted([(0, 0)], False, [])
+    across, partial = lax.optimization_barrier((across, partial))
+    quarters += [across, swap(across, 1)]
+    partial = contracted([(1, 0), (2, 0)], False, [partial])
     partial = contracted([(0, 1), (1, 1), (2, 1), (3, 0), (3, 1)], True, [partial])
     parts = lax.all_to_all(
         partial.astype(SEND_TYPE).reshape(near, rows, FOLD),

time: 65.5 us -> 65 us (level)
  waiting for transfers between devices: 21.8 us -> 20.8 us
    ppermute x5, waiting for transfers between devices: 10.8 us -> 10.1 us  [swap(): return lax.ppermute(x, 'col', [(m, m ^ p) for m in range(4)])]
    pallas_call x2 -> x3, Pallas kernels: 3.14 us -> 3.65 us  [contracted(): pl.pallas_call(functools.partial(contract, terms, last), out_shape=jax.Sh...]
  transfers between devices with their start and end apart: 7 -> 7, of which waited for: 5 -> 5; matrix products, arithmetic and copies ran while one was open for 0% -> 0% of each run, Pallas kernels for 11% -> 12%
where the time goes in v4:
time: 65 us; the launch traced here: 64.5 us
  blocking collectives  21.4 us (33%)
  waiting for transfers between devices  20.8 us (32%)
  Pallas kernels  11.9 us (18%)
  starting transfers between devices  9.34 us (14%)
  other arithmetic  0.82 us (1%)
    all_to_all x1, blocking collectives, local(): lax.all_to_all(turned, 'row', split_axis=0, concat_axis=0, tiled=True, ax...  21.4 us
    all_to_all x1, waiting for transfers between devices, local(): lax.all_to_all(partial.astype(SEND_TYPE).reshape(near, rows, FOLD), 'row'...  10.7 us
    ppermute x5, waiting for transfers between devices, swap(): return lax.ppermute(x, 'col', [(m, m ^ p) for m in range(4)])  10.1 us
    all_to_all x1, starting transfers between devices, local(): lax.all_to_all(partial.astype(SEND_TYPE).reshape(near, rows, FOLD), 'row'...  4.82 us
    pallas_call x3, Pallas kernels, contracted(): pl.pallas_call(functools.partial(contract, terms, last), out_shape=jax.Sh...  3.65 us
    pallas_call x1, Pallas kernels, local(): pl.pallas_call(fold_integrals, out_shape=[jax.ShapeDtypeStruct((occ_local...  3.2 us
    ppermute x5, starting transfers between devices, swap(): return lax.ppermute(x, 'col', [(m, m ^ p) for m in range(4)])  3.16 us
    pallas_call x2, Pallas kernels, folded(): pl.pallas_call(functools.partial(fold_amplitudes, odd), out_shape=jax.Sha...  3.02 us
  transfers between devices with their start and end apart: 7, of which 5 were waited for; matrix products, arithmetic and copies ran while one was open for 0% of the time, Pallas kernels for 12%

profile of v4, /device:TPU:4, one launch (start us, length us, event | category | flops | bytes accessed | tf_op | source)
XLA Modules:
  0.0 64.5 jit_solution(11974726810166660426)
XLA Ops:
  0.0 1.5 %fold_amplitudes.2.after_hbm = bf16[2,64,16,128]{3,2,1,0:T(8,128)(2,1)S(1)} custom-call(bf16[300,16,128]{2,1,0:T(8,128)(2,1)} %bitcast.7, s32[1,128]{1,0:T(1,128)} %bitcast.5, s32[128]{0:T(128)} %occ_ref.1, s32[1200]{0:T(1024)} %vir_ref.1, s32[128]{0:T(128)} %occ_ref.1), custom_call_target="tpu_custom_call" | custom-call | tf_op jit(solution)/shard_map/fold_amplitudes/pallas_call | solution.py:265
  1.5 0.1 collective-permute-start
  1.6 1.5 %fold_amplitudes.3.a_ref = bf16[2,64,16,128]{3,2,1,0:T(8,128)(2,1)S(1)} custom-call(bf16[300,16,128]{2,1,0:T(8,128)(2,1)} %bitcast.8, s32[1,128]{1,0:T(1,128)} %bitcast.6, s32[128]{0:T(128)} %occ_ref.1, s32[1200]{0:T(1024)} %vir_ref.1, bf16[2,64,16,128]{3,2,1,0:T(8,128)(2,1)S(1)} %fold_amplitudes.2.after_hbm), custom_call_target="tpu_custom_call" | custom-call | tf_op jit(solution)/shard_map/fold_amplitudes/pallas_call | solution.py:265
  3.1 0.4 collective-permute-done.b_ref
  3.6 2.3 %collective-permute-start.1 = (bf16[64,16,128]{2,1,0:T(8,128)(2,1)S(1)}, bf16[64,16,128]{2,1,0:T(8,128)(2,1)S(1)}, u32[]{:S(2)}, u32[]{:S(2)}) collective-permute-start(bf16[64,16,128]{2,1,0:T(8,128)(2,1)S(1)} %fusion.after_hbm), channel_id=1, source_target_pairs={{0,2},{1,3},{2,0},{3,1},{4,6},{5,7},{6,4},{7,5},{8,10},{9,11},{10,... | collective-permute-start | bytes 786440 | tf_op jit(solution)/shard_map/ppermute | solution.py:292
  5.9 3.2 %fold_integrals.1 = (bf16[2,1216,256]{2,1,0:T(8,128)(2,1)S(1)}, bf16[1200,128]{1,0:T(8,128)(2,1)S(1)}, s32[1,1200]{1,0:T(1,128)S(1)}, s32[20,128]{1,0:T(8,128)S(1)}) custom-call(bf16[2,1200,1200]{2,1,0:T(8,128)(2,1)} %int_hbm.1, s32[128]{0:T(128)} %occ_ref.1, s32[1200]{0:T(1024)} %vir_ref.1, bf16[64,16,128]{2,1,0:T(8,128)(2,1)S(1)} %fusion.after_hbm), custom_call_target="tpu_custom_call" | custom-call | tf_op jit(solution)/shard_map/fold_integrals/pallas_call | solution.py:296
  9.1 0.0 copy-start.2
  9.1 1.4 %collective-permute-start.5 = (bf16[2,1216,256]{2,1,0:T(8,128)(2,1)S(1)}, bf16[2,1216,256]{2,1,0:T(8,128)(2,1)S(1)}, u32[]{:S(2)}, u32[]{:S(2)}) collective-permute-start(bf16[2,1216,256]{2,1,0:T(8,128)(2,1)S(1)} %get-tuple-element.13.refs_1_.refs_2_.refs_4_), channel_id=1, source_target_pairs={{0,192},{4,196},{8,200},{12,204},{16,208},{20,212},{24,216},{28,22... | collective-permute-start | bytes 3735560 | tf_op jit(solution)/shard_map/ppermute | solution.py:339
  10.5 3.1 %collective-permute-done.1.c_ref = bf16[64,16,128]{2,1,0:T(8,128)(2,1)S(1)} collective-permute-done((bf16[64,16,128]{2,1,0:T(8,128)(2,1)S(1)}, bf16[64,16,128]{2,1,0:T(8,128)(2,1)S(1)}, u32[]{:S(2)}, u32[]{:S(2)}) %collective-permute-start.1) | collective-permute-done | bytes 262176 | tf_op jit(solution)/shard_map/ppermute | solution.py:292
  13.5 0.6 turn_amplitudes.1
  14.1 21.4 %all_to_all.10.refs_0_ = bf16[32,2,16,128]{3,2,1,0:T(8,128)(2,1)S(1)} all-to-all(bf16[32,2,16,128]{3,2,1,0:T(8,128)(2,1)S(1)} %turn_amplitudes.1), channel_id=1, replica_groups={{0,4,8,12,16,20,24,28,32,36,40,44,48,52,56,60,64,68,72,76,80,84,88,92,9..., dimensions={0} | all-to-all | bytes 524288 | tf_op jit(solution)/shard_map/all_to_all | solution.py:336
  35.5 0.8 %collective-permute-start.3 = (bf16[32,2,16,128]{3,2,1,0:T(8,128)(2,1)S(1)}, bf16[32,2,16,128]{3,2,1,0:T(8,128)(2,1)S(1)}, u32[]{:S(2)}, u32[]{:S(2)}) collective-permute-start(bf16[32,2,16,128]{3,2,1,0:T(8,128)(2,1)S(1)} %all_to_all.10.refs_0_), channel_id=1, source_target_pairs={{0,2},{1,3},{2,0},{3,1},{4,6},{5,7},{6,4},{7,5},{8,10},{9,11},{10,... | collective-permute-start | bytes 786440 | tf_op jit(solution)/shard_map/ppermute | solution.py:292
  36.3 0.0 collective-permute-start.2
  36.3 0.0 copy-done.2
  36.3 0.9 %contract.3.refs_6_ = f32[512,256]{1,0:T(8,128)S(1)} custom-call(bf16[32,2,16,128]{3,2,1,0:T(8,128)(2,1)S(1)} %all_to_all.10.refs_0_, bf16[2,1216,256]{2,1,0:T(8,128)(2,1)S(1)} %get-tuple-element.13.refs_1_.refs_2_.refs_4_, bf16[1200,128]{1,0:T(8,128)(2,1)S(1)} %get-tuple-element.14.refs_2_.refs_3_.refs_6_, ...), custom_call_target="tpu_custom_call" | custom-call | tf_op jit(solution)/shard_map/contract/pallas_call | solution.py:344
  37.3 6.2 %collective-permute-done.3.refs_1_.refs_2_ = bf16[32,2,16,128]{3,2,1,0:T(8,128)(2,1)S(1)} collective-permute-done((bf16[32,2,16,128]{3,2,1,0:T(8,128)(2,1)S(1)}, bf16[32,2,16,128]{3,2,1,0:T(8,128)(2,1)S(1)}, u32[]{:S(2)}, u32[]{:S(2)}) %collective-permute-start.3) | collective-permute-done | bytes 262176 | tf_op jit(solution)/shard_map/ppermute | solution.py:292
  43.4 0.0 collective-permute-start.4
  43.4 0.0 collective-permute-done.2.refs_0_.refs_1_
  43.4 1.1 %contract.4.refs_9_ = f32[512,256]{1,0:T(8,128)S(1)} custom-call(bf16[32,2,16,128]{3,2,1,0:T(8,128)(2,1)S(1)} %collective-permute-done.2.refs_0_.refs_1_, bf16[32,2,16,128]{3,2,1,0:T(8,128)(2,1)S(1)} %collective-permute-done.3.refs_1_.refs_2_, bf16[2,1216,256]{2,1,0:T(8,128)(2,1)S(1)} %get-tuple-element.13.refs_1_.refs_2_.refs_4_, ...), custom_call_target="tpu_custom_call" | custom-call | tf_op jit(solution)/shard_map/contract/pallas_call | solution.py:344
  44.5 0.0 collective-permute-done.5.refs_5_
  44.5 0.4 collective-permute-done.4.refs_3_
  45.0 1.7 %contract.5 = f32[512,256]{1,0:T(8,128)S(1)} custom-call(bf16[32,2,16,128]{3,2,1,0:T(8,128)(2,1)S(1)} %all_to_all.10.refs_0_, bf16[32,2,16,128]{3,2,1,0:T(8,128)(2,1)S(1)} %collective-permute-done.2.refs_0_.refs_1_, bf16[32,2,16,128]{3,2,1,0:T(8,128)(2,1)S(1)} %collective-permute-done.3.refs_1_.refs_2_, ...), custom_call_target="tpu_custom_call" | custom-call | tf_op jit(solution)/shard_map/contract/pallas_call | solution.py:344
  46.6 0.0 copy-start.3
  46.6 0.0 copy-start
  46.6 0.0 copy-start.1
  46.7 0.0 copy-start.4
  46.7 0.7 %convert_element_type.6 = f16[512,256]{1,0:T(8,128)(2,1)} convert(f32[512,256]{1,0:T(8,128)S(1)} %contract.5) | non-fusion elementwise | flops 131072 | bytes 786432 | tf_op jit(solution)/shard_map/convert_element_type | solution.py:360
  47.4 4.8 %all-to-all-start.1 = ((f16[32,16,256]{2,1,0:T(8,128)(2,1)}), f16[32,16,256]{2,1,0:T(8,128)(2,1)S(1)}, u32[]{:S(2)}, u32[]{:S(2)}) async-start(f16[32,16,256]{2,1,0:T(8,128)(2,1)} %bitcast.3), calls=%async_computation.1 | async-start | bytes 524288 | tf_op jit(solution)/shard_map/all_to_all | solution.py:359
  52.2 0.0 copy-done.3
  52.3 0.8 %prepare.1 = (f32[16,1200]{1,0:T(8,128)S(1)}, f32[16,1200]{1,0:T(8,128)S(1)}) custom-call(f32[16,1200]{1,0:T(8,128)S(1)} %copy-done.1, s32[1,1200]{1,0:T(1,128)S(1)} %get-tuple-element.18.vir_vec_ref, f32[1,1200]{1,0:T(1,128)S(1)} %reshape.12.energy_vec_ref, s32[128]{0:T(128)S(1)} %copy-done.2, s32[1200]{0:T(1024)S(1)} %copy-done, f32[128]{0:T(128)S(1)} %copy-done.4, ...), custom_call_target="tpu_custom_call" | custom-call | tf_op jit(solution)/shard_map/prepare/pallas_call | solution.py:367
  53.1 10.7 %all-to-all-done.1 = f16[32,16,256]{2,1,0:T(8,128)(2,1)S(1)} async-done(((f16[32,16,256]{2,1,0:T(8,128)(2,1)}), f16[32,16,256]{2,1,0:T(8,128)(2,1)S(1)}, u32[]{:S(2)}, u32[]{:S(2)}) %all-to-all-start.1) | async-done | bytes 262176 | tf_op jit(solution)/shard_map/all_to_all | solution.py:359
  63.8 0.6 %finish.1 = f32[16,1200]{1,0:T(8,128)} custom-call(f32[16,256]{1,0:T(8,128)S(1)} %convert_reduce_fusion.part_ref, f32[16,1200]{1,0:T(8,128)S(1)} %get-tuple-element.19.plain_ref, f32[16,1200]{1,0:T(8,128)S(1)} %get-tuple-element.20.factor_ref), custom_call_target="tpu_custom_call" | custom-call | tf_op jit(solution)/shard_map/finish/pallas_call | solution.py:383
  (6 shorter events, 0.1 us)
Async XLA Ops:
  1.5 2.0 %collective-permute-start = (bf16[2,64,16,128]{3,2,1,0:T(8,128)(2,1)S(1)}, bf16[2,64,16,128]{3,2,1,0:T(8,128)(2,1)S(1)}, u32[]{:S(2)}, u32[]{:S(2)}) collective-permute-start(bf16[2,64,16,128]{3,2,1,0:T(8,128)(2,1)S(1)} %fold_amplitudes.2.after_hbm), channel_id=1, source_target_pairs={{0,1},{1,0},{2,3},{3,2},{4,5},{5,4},{6,7},{7,6},{8,9},{9,8},{10,11... | collective-permute-start | bytes 1572872 | tf_op jit(solution)/shard_map/ppermute | solution.py:292
  3.6 9.9 %collective-permute-start.1 = (bf16[64,16,128]{2,1,0:T(8,128)(2,1)S(1)}, bf16[64,16,128]{2,1,0:T(8,128)(2,1)S(1)}, u32[]{:S(2)}, u32[]{:S(2)}) collective-permute-start(bf16[64,16,128]{2,1,0:T(8,128)(2,1)S(1)} %fusion.after_hbm), channel_id=1, source_target_pairs={{0,2},{1,3},{2,0},{3,1},{4,6},{5,7},{6,4},{7,5},{8,10},{9,11},{10,... | collective-permute-start | bytes 786440 | tf_op jit(solution)/shard_map/ppermute | solution.py:292
  9.1 27.2 %copy-start.2 = (s32[128]{0:T(128)S(1)}, s32[128]{0:T(128)}, u32[]{:S(2)}) copy-start(s32[128]{0:T(128)} %occ_ref.1) | copy-start | bytes 1540
  9.1 35.4 %collective-permute-start.5 = (bf16[2,1216,256]{2,1,0:T(8,128)(2,1)S(1)}, bf16[2,1216,256]{2,1,0:T(8,128)(2,1)S(1)}, u32[]{:S(2)}, u32[]{:S(2)}) collective-permute-start(bf16[2,1216,256]{2,1,0:T(8,128)(2,1)S(1)} %get-tuple-element.13.refs_1_.refs_2_.refs_4_), channel_id=1, source_target_pairs={{0,192},{4,196},{8,200},{12,204},{16,208},{20,212},{24,216},{28,22... | collective-permute-start | bytes 3735560 | tf_op jit(solution)/shard_map/ppermute | solution.py:339
  35.5 7.9 %collective-permute-start.3 = (bf16[32,2,16,128]{3,2,1,0:T(8,128)(2,1)S(1)}, bf16[32,2,16,128]{3,2,1,0:T(8,128)(2,1)S(1)}, u32[]{:S(2)}, u32[]{:S(2)}) collective-permute-start(bf16[32,2,16,128]{3,2,1,0:T(8,128)(2,1)S(1)} %all_to_all.10.refs_0_), channel_id=1, source_target_pairs={{0,2},{1,3},{2,0},{3,1},{4,6},{5,7},{6,4},{7,5},{8,10},{9,11},{10,... | collective-permute-start | bytes 786440 | tf_op jit(solution)/shard_map/ppermute | solution.py:292
  36.3 7.1 %collective-permute-start.2 = (bf16[32,2,16,128]{3,2,1,0:T(8,128)(2,1)S(1)}, bf16[32,2,16,128]{3,2,1,0:T(8,128)(2,1)S(1)}, u32[]{:S(2)}, u32[]{:S(2)}) collective-permute-start(bf16[32,2,16,128]{3,2,1,0:T(8,128)(2,1)S(1)} %all_to_all.10.refs_0_), channel_id=1, source_target_pairs={{0,1},{1,0},{2,3},{3,2},{4,5},{5,4},{6,7},{7,6},{8,9},{9,8},{10,11... | collective-permute-start | bytes 786440 | tf_op jit(solution)/shard_map/ppermute | solution.py:292
  43.4 1.5 %collective-permute-start.4 = (bf16[32,2,16,128]{3,2,1,0:T(8,128)(2,1)S(1)}, bf16[32,2,16,128]{3,2,1,0:T(8,128)(2,1)S(1)}, u32[]{:S(2)}, u32[]{:S(2)}) collective-permute-start(bf16[32,2,16,128]{3,2,1,0:T(8,128)(2,1)S(1)} %collective-permute-done.3.refs_1_.refs_2_), channel_id=1, source_target_pairs={{0,1},{1,0},{2,3},{3,2},{4,5},{5,4},{6,7},{7,6},{8,9},{9,8},{10,11... | collective-permute-start | bytes 786440 | tf_op jit(solution)/shard_map/ppermute | solution.py:292
  46.6 5.6 %copy-start.3 = (f32[1200]{0:T(1024)S(1)}, f32[1200]{0:T(1024)}, u32[]{:S(2)}) copy-start(f32[1200]{0:T(1024)} %vir_e_ref.1) | copy-start | bytes 14404
  46.6 5.6 %copy-start = (s32[1200]{0:T(1024)S(1)}, s32[1200]{0:T(1024)}, u32[]{:S(2)}) copy-start(s32[1200]{0:T(1024)} %vir_ref.1) | copy-start | bytes 14404
  46.6 5.6 %copy-start.1 = (f32[16,1200]{1,0:T(8,128)S(1)}, f32[16,1200]{1,0:T(8,128)}, u32[]{:S(2)}) copy-start(f32[16,1200]{1,0:T(8,128)} %res_ref.1) | copy-start | bytes 230404
  46.7 5.6 %copy-start.4 = (f32[128]{0:T(128)S(1)}, f32[128]{0:T(128)}, u32[]{:S(2)}) copy-start(f32[128]{0:T(128)} %occ_e_ref.1) | copy-start | bytes 1540
  47.4 16.4 %all-to-all-start.1 = ((f16[32,16,256]{2,1,0:T(8,128)(2,1)}), f16[32,16,256]{2,1,0:T(8,128)(2,1)S(1)}, u32[]{:S(2)}, u32[]{:S(2)}) async-start(f16[32,16,256]{2,1,0:T(8,128)(2,1)} %bitcast.3), calls=%async_computation.1 | async-start | bytes 524288 | tf_op jit(solution)/shard_map/all_to_all | solution.py:359

commit v5 on v4

--- a/solution.py
+++ b/solution.py
@@ -149,14 +149,20 @@
         lab_ref[c : c + 80, :] = labels_of(at).astype(jnp.bfloat16)
     vir_vec = labels_of(lax.broadcasted_iota(jnp.int32, (1, width), 1))
     vec_ref[...] = vir_vec
-    for block in range(tab_ref.shape[0]):
+    high = lax.broadcasted_iota(jnp.int32, (1, 2 * QUARTER), 1) >= QUARTER
+    wanted = []
+    for partner in PARTNERS:
+        other = 2 * (lax.axis_index("row") ^ partner)
+        wanted.append(jnp.where(high, occ_ref[other + 1], occ_ref[other]) ^ occ_ref[0])
+    for block in range(tab_ref.shape[1]):
         size = min(QUARTER, v - block * QUARTER)
         x = jnp.full((1, QUARTER), 64, jnp.int32)
         if size > 0:
             x = vir_vec[:, block * QUARTER : block * QUARTER + size]
             if size < QUARTER:
                 x = jnp.concatenate([x, jnp.full((1, QUARTER - size), 64, jnp.int32)], axis=1)
-        tab_ref[block : block + 1, :] = jnp.concatenate([x, x], axis=1)
+        for d in range(FAR):
+            tab_ref[d, block : block + 1, :] = jnp.concatenate([x, x], axis=1) ^ wanted[d]
     for k in range(2):
         label = occ_ref[lax.axis_index("row") * 2 + k] ^ occ_ref[1 + lax.axis_index("col")]
         b_labels = (vir_vec ^ label).astype(jnp.bfloat16)
@@ -182,28 +188,24 @@
     quarters, partners = sorted({p for p, _ in terms}), sorted({d for _, d in terms})
     cut = len(quarters) + len(partners)
     t_refs, w_refs = refs[: len(quarters)], refs[len(quarters) : cut]
-    lab_ref, tab_ref, occ_ref = refs[cut : cut + 3]
-    sum_refs, (out_ref, a_lab_ref) = refs[cut + 3 : -2], refs[-2:]
+    lab_ref, tab_ref = refs[cut : cut + 2]
+    sum_refs, (out_ref, a_lab_ref) = refs[cut + 2 : -2], refs[-2:]
     near, far, rows, lanes = t_refs[0].shape
     tall = w_refs[0].shape[1]
     me = lax.axis_index("col")
-    own = lax.axis_index("row")
     shift = own_shift()
     for i, member in enumerate(SAME):
         label = lab_ref[pl.ds(pl.multiple_of((member ^ shift) * rows, rows), rows), :]
         a_lab_ref[i * rows : (i + 1) * rows, :] = label
-    high = lax.broadcasted_iota(jnp.int32, (1, lanes), 1) >= QUARTER
     a_labels = a_lab_ref[...]
     total = sum_refs[0][...] if sum_refs else None
-    blocks = [(p, d, t) for p, d in terms for t in range(tab_ref.shape[0] // 4)]
+    blocks = [(p, d, t) for p, d in terms for t in range(tab_ref.shape[1] // 4)]
     for n in range(0, len(blocks), 2):
         lhs, w = [], []
         for p, d, t in blocks[n : n + 2]:
-            other = 2 * (own ^ PARTNERS[d])
-            wanted = jnp.where(high, occ_ref[other + 1], occ_ref[other]) ^ occ_ref[0]
             block = 4 * t + (me ^ p)
             x = t_refs[quarters.index(p)][:, d].reshape(near * rows, lanes)
-            c_labels = (tab_ref[pl.ds(block, 1), :] ^ wanted).astype(jnp.bfloat16)
+            c_labels = tab_ref[d, pl.ds(block, 1), :].astype(jnp.bfloat16)
             lhs.append(jnp.where(a_labels == c_labels, x, jnp.zeros_like(x)))
             c = pl.multiple_of(jnp.minimum(block * QUARTER, tall - QUARTER), QUARTER)
             w += [w_refs[partners.index(d)][k, pl.ds(c, QUARTER), :] for k in range(2)]
@@ -299,7 +301,7 @@
             jax.ShapeDtypeStruct((occ_local, -(-v // QUARTER) * QUARTER, FOLD), jnp.bfloat16),
             jax.ShapeDtypeStruct((v, 128), jnp.bfloat16),
             jax.ShapeDtypeStruct((1, v), jnp.int32),
-            jax.ShapeDtypeStruct((4 * (-(-v // FOLD)), 2 * QUARTER), jnp.int32),
+            jax.ShapeDtypeStruct((FAR, 4 * (-(-v // FOLD)), 2 * QUARTER), jnp.int32),
         ],
         in_specs=[hbm] * 4,
         out_specs=[vmem] * 4,
@@ -344,12 +346,12 @@
         return pl.pallas_call(
             functools.partial(contract, terms, last),
             out_shape=jax.ShapeDtypeStruct((near * rows, FOLD), jnp.float32),
-            in_specs=[vmem] * (len(used) + 2) + [smem] + [vmem] * len(sums),
+            in_specs=[vmem] * (len(used) + 2 + len(sums)),
             out_specs=vmem,
             scratch_shapes=[pltpu.VMEM((near * rows, occ_local * QUARTER), jnp.bfloat16)],
             compiler_params=big,
             name="contract",
-        )(*used, labels, table, occupied_irrep, *sums)
+        )(*used, labels, table, *sums)
 
     partial = contracted([(0, 0)], False, [])
     across, partial = lax.optimization_barrier((across, partial))

time: 65 us -> 64.5 us (level)
  Pallas kernels: 11.9 us -> 10.2 us
  waiting for transfers between devices: 20.8 us -> 21.9 us
    pallas_call x3, Pallas kernels: 3.65 us -> 1.99 us  [contracted(): pl.pallas_call(functools.partial(contract, terms, last), out_shape=jax.Sh...]
    ppermute x5, waiting for transfers between devices: 10.1 us -> 11.2 us  [swap(): return lax.ppermute(x, 'col', [(m, m ^ p) for m in range(4)])]
  transfers between devices with their start and end apart: 7 -> 7, of which waited for: 5 -> 5; matrix products, arithmetic and copies ran while one was open for 0% -> 0% of each run, Pallas kernels for 12% -> 11%
where the time goes in v5:
time: 64.5 us; the launch traced here: 64 us
  waiting for transfers between devices  21.9 us (34%)
  blocking collectives  21.4 us (33%)
  Pallas kernels  10.2 us (16%)
  starting transfers between devices  9.33 us (14%)
  other arithmetic  0.82 us (1%)
    all_to_all x1, blocking collectives, local(): lax.all_to_all(turned, 'row', split_axis=0, concat_axis=0, tiled=True, ax...  21.4 us
    ppermute x5, waiting for transfers between devices, swap(): return lax.ppermute(x, 'col', [(m, m ^ p) for m in range(4)])  11.2 us
    all_to_all x1, waiting for transfers between devices, local(): lax.all_to_all(partial.astype(SEND_TYPE).reshape(near, rows, FOLD), 'row'...  10.7 us
    all_to_all x1, starting transfers between devices, local(): lax.all_to_all(partial.astype(SEND_TYPE).reshape(near, rows, FOLD), 'row'...  4.81 us
    pallas_call x1, Pallas kernels, local(): pl.pallas_call(fold_integrals, out_shape=[jax.ShapeDtypeStruct((occ_local...  3.22 us
    ppermute x5, starting transfers between devices, swap(): return lax.ppermute(x, 'col', [(m, m ^ p) for m in range(4)])  3.16 us
    pallas_call x2, Pallas kernels, folded(): pl.pallas_call(functools.partial(fold_amplitudes, odd), out_shape=jax.Sha...  3.02 us
    pallas_call x3, Pallas kernels, contracted(): pl.pallas_call(functools.partial(contract, terms, last), out_shape=jax.Sh...  1.99 us
  transfers between devices with their start and end apart: 7, of which 5 were waited for; matrix products, arithmetic and copies ran while one was open for 0% of the time, Pallas kernels for 11%

profile of v5, /device:TPU:4, one launch (start us, length us, event | category | flops | bytes accessed | tf_op | source)
XLA Modules:
  0.0 64.0 jit_solution(16002747600748611784)
XLA Ops:
  0.0 1.5 %fold_amplitudes.2.after_hbm = bf16[2,64,16,128]{3,2,1,0:T(8,128)(2,1)S(1)} custom-call(bf16[300,16,128]{2,1,0:T(8,128)(2,1)} %bitcast.7, s32[1,128]{1,0:T(1,128)} %bitcast.5, s32[128]{0:T(128)} %occ_ref.1, s32[1200]{0:T(1024)} %vir_ref.1, s32[128]{0:T(128)} %occ_ref.1), custom_call_target="tpu_custom_call" | custom-call | tf_op jit(solution)/shard_map/fold_amplitudes/pallas_call | solution.py:267
  1.5 0.1 collective-permute-start
  1.6 1.5 %fold_amplitudes.3.a_ref = bf16[2,64,16,128]{3,2,1,0:T(8,128)(2,1)S(1)} custom-call(bf16[300,16,128]{2,1,0:T(8,128)(2,1)} %bitcast.8, s32[1,128]{1,0:T(1,128)} %bitcast.6, s32[128]{0:T(128)} %occ_ref.1, s32[1200]{0:T(1024)} %vir_ref.1, bf16[2,64,16,128]{3,2,1,0:T(8,128)(2,1)S(1)} %fold_amplitudes.2.after_hbm), custom_call_target="tpu_custom_call" | custom-call | tf_op jit(solution)/shard_map/fold_amplitudes/pallas_call | solution.py:267
  3.1 0.4 collective-permute-done.b_ref
  3.6 2.3 %collective-permute-start.1 = (bf16[64,16,128]{2,1,0:T(8,128)(2,1)S(1)}, bf16[64,16,128]{2,1,0:T(8,128)(2,1)S(1)}, u32[]{:S(2)}, u32[]{:S(2)}) collective-permute-start(bf16[64,16,128]{2,1,0:T(8,128)(2,1)S(1)} %fusion.after_hbm), channel_id=1, source_target_pairs={{0,2},{1,3},{2,0},{3,1},{4,6},{5,7},{6,4},{7,5},{8,10},{9,11},{10,... | collective-permute-start | bytes 786440 | tf_op jit(solution)/shard_map/ppermute | solution.py:294
  5.9 3.2 %fold_integrals.1 = (bf16[2,1216,256]{2,1,0:T(8,128)(2,1)S(1)}, bf16[1200,128]{1,0:T(8,128)(2,1)S(1)}, s32[1,1200]{1,0:T(1,128)S(1)}, s32[2,20,128]{2,1,0:T(8,128)S(1)}) custom-call(bf16[2,1200,1200]{2,1,0:T(8,128)(2,1)} %int_hbm.1, s32[128]{0:T(128)} %occ_ref.1, s32[1200]{0:T(1024)} %vir_ref.1, bf16[64,16,128]{2,1,0:T(8,128)(2,1)S(1)} %fusion.after_hbm), custom_call_target="tpu_custom_call" | custom-call | tf_op jit(solution)/shard_map/fold_integrals/pallas_call | solution.py:298
  9.1 1.4 %collective-permute-start.5 = (bf16[2,1216,256]{2,1,0:T(8,128)(2,1)S(1)}, bf16[2,1216,256]{2,1,0:T(8,128)(2,1)S(1)}, u32[]{:S(2)}, u32[]{:S(2)}) collective-permute-start(bf16[2,1216,256]{2,1,0:T(8,128)(2,1)S(1)} %get-tuple-element.13.refs_1_.refs_2_.refs_4_), channel_id=1, source_target_pairs={{0,192},{4,196},{8,200},{12,204},{16,208},{20,212},{24,216},{28,22... | collective-permute-start | bytes 3735560 | tf_op jit(solution)/shard_map/ppermute | solution.py:341
  10.5 3.1 %collective-permute-done.1.c_ref = bf16[64,16,128]{2,1,0:T(8,128)(2,1)S(1)} collective-permute-done((bf16[64,16,128]{2,1,0:T(8,128)(2,1)S(1)}, bf16[64,16,128]{2,1,0:T(8,128)(2,1)S(1)}, u32[]{:S(2)}, u32[]{:S(2)}) %collective-permute-start.1) | collective-permute-done | bytes 262176 | tf_op jit(solution)/shard_map/ppermute | solution.py:294
  13.5 0.6 turn_amplitudes.1
  14.1 21.4 %all_to_all.10.refs_0_ = bf16[32,2,16,128]{3,2,1,0:T(8,128)(2,1)S(1)} all-to-all(bf16[32,2,16,128]{3,2,1,0:T(8,128)(2,1)S(1)} %turn_amplitudes.1), channel_id=1, replica_groups={{0,4,8,12,16,20,24,28,32,36,40,44,48,52,56,60,64,68,72,76,80,84,88,92,9..., dimensions={0} | all-to-all | bytes 524288 | tf_op jit(solution)/shard_map/all_to_all | solution.py:338
  35.6 0.8 %collective-permute-start.3 = (bf16[32,2,16,128]{3,2,1,0:T(8,128)(2,1)S(1)}, bf16[32,2,16,128]{3,2,1,0:T(8,128)(2,1)S(1)}, u32[]{:S(2)}, u32[]{:S(2)}) collective-permute-start(bf16[32,2,16,128]{3,2,1,0:T(8,128)(2,1)S(1)} %all_to_all.10.refs_0_), channel_id=1, source_target_pairs={{0,2},{1,3},{2,0},{3,1},{4,6},{5,7},{6,4},{7,5},{8,10},{9,11},{10,... | collective-permute-start | bytes 786440 | tf_op jit(solution)/shard_map/ppermute | solution.py:294
  36.3 0.0 collective-permute-start.2
  36.3 0.4 contract.3.refs_5_
  36.7 6.7 %collective-permute-done.3.refs_1_.refs_2_ = bf16[32,2,16,128]{3,2,1,0:T(8,128)(2,1)S(1)} collective-permute-done((bf16[32,2,16,128]{3,2,1,0:T(8,128)(2,1)S(1)}, bf16[32,2,16,128]{3,2,1,0:T(8,128)(2,1)S(1)}, u32[]{:S(2)}, u32[]{:S(2)}) %collective-permute-start.3) | collective-permute-done | bytes 262176 | tf_op jit(solution)/shard_map/ppermute | solution.py:294
  43.4 0.0 collective-permute-start.4
  43.4 0.0 collective-permute-done.2.refs_0_.refs_1_
  43.4 0.5 contract.4.refs_8_
  44.0 0.0 collective-permute-done.5.refs_5_
  44.0 1.0 %collective-permute-done.4.refs_3_ = bf16[32,2,16,128]{3,2,1,0:T(8,128)(2,1)S(1)} collective-permute-done((bf16[32,2,16,128]{3,2,1,0:T(8,128)(2,1)S(1)}, bf16[32,2,16,128]{3,2,1,0:T(8,128)(2,1)S(1)}, u32[]{:S(2)}, u32[]{:S(2)}) %collective-permute-start.4) | collective-permute-done | bytes 262176 | tf_op jit(solution)/shard_map/ppermute | solution.py:294
  45.0 1.1 %contract.5 = f32[512,256]{1,0:T(8,128)S(1)} custom-call(bf16[32,2,16,128]{3,2,1,0:T(8,128)(2,1)S(1)} %all_to_all.10.refs_0_, bf16[32,2,16,128]{3,2,1,0:T(8,128)(2,1)S(1)} %collective-permute-done.2.refs_0_.refs_1_, bf16[32,2,16,128]{3,2,1,0:T(8,128)(2,1)S(1)} %collective-permute-done.3.refs_1_.refs_2_, ...), custom_call_target="tpu_custom_call" | custom-call | tf_op jit(solution)/shard_map/contract/pallas_call | solution.py:346
  46.1 0.0 copy-start.2
  46.1 0.0 copy-start
  46.1 0.0 copy-start.1
  46.1 0.0 copy-start.3
  46.1 0.0 copy-start.4
  46.1 0.7 %convert_element_type.6 = f16[512,256]{1,0:T(8,128)(2,1)} convert(f32[512,256]{1,0:T(8,128)S(1)} %contract.5) | non-fusion elementwise | flops 131072 | bytes 786432 | tf_op jit(solution)/shard_map/convert_element_type | solution.py:362
  46.9 4.8 %all-to-all-start.1 = ((f16[32,16,256]{2,1,0:T(8,128)(2,1)}), f16[32,16,256]{2,1,0:T(8,128)(2,1)S(1)}, u32[]{:S(2)}, u32[]{:S(2)}) async-start(f16[32,16,256]{2,1,0:T(8,128)(2,1)} %bitcast.3), calls=%async_computation.1 | async-start | bytes 524288 | tf_op jit(solution)/shard_map/all_to_all | solution.py:361
  51.7 0.0 copy-done.2
  51.7 0.0 copy-done
  51.7 0.8 %prepare.1 = (f32[16,1200]{1,0:T(8,128)S(1)}, f32[16,1200]{1,0:T(8,128)S(1)}) custom-call(f32[16,1200]{1,0:T(8,128)S(1)} %copy-done.1, s32[1,1200]{1,0:T(1,128)S(1)} %get-tuple-element.18.vir_vec_ref, f32[1,1200]{1,0:T(1,128)S(1)} %reshape.12.energy_vec_ref, s32[128]{0:T(128)S(1)} %copy-done.3, s32[1200]{0:T(1024)S(1)} %copy-done, f32[128]{0:T(128)S(1)} %copy-done.4, ...), custom_call_target="tpu_custom_call" | custom-call | tf_op jit(solution)/shard_map/prepare/pallas_call | solution.py:369
  52.5 10.7 %all-to-all-done.1 = f16[32,16,256]{2,1,0:T(8,128)(2,1)S(1)} async-done(((f16[32,16,256]{2,1,0:T(8,128)(2,1)}), f16[32,16,256]{2,1,0:T(8,128)(2,1)S(1)}, u32[]{:S(2)}, u32[]{:S(2)}) %all-to-all-start.1) | async-done | bytes 262176 | tf_op jit(solution)/shard_map/all_to_all | solution.py:361
  63.3 0.6 %finish.1 = f32[16,1200]{1,0:T(8,128)} custom-call(f32[16,256]{1,0:T(8,128)S(1)} %convert_reduce_fusion.part_ref, f32[16,1200]{1,0:T(8,128)S(1)} %get-tuple-element.19.plain_ref, f32[16,1200]{1,0:T(8,128)S(1)} %get-tuple-element.20.factor_ref), custom_call_target="tpu_custom_call" | custom-call | tf_op jit(solution)/shard_map/finish/pallas_call | solution.py:385
  (6 shorter events, 0.1 us)
Async XLA Ops:
  1.5 2.0 %collective-permute-start = (bf16[2,64,16,128]{3,2,1,0:T(8,128)(2,1)S(1)}, bf16[2,64,16,128]{3,2,1,0:T(8,128)(2,1)S(1)}, u32[]{:S(2)}, u32[]{:S(2)}) collective-permute-start(bf16[2,64,16,128]{3,2,1,0:T(8,128)(2,1)S(1)} %fold_amplitudes.2.after_hbm), channel_id=1, source_target_pairs={{0,1},{1,0},{2,3},{3,2},{4,5},{5,4},{6,7},{7,6},{8,9},{9,8},{10,11... | collective-permute-start | bytes 1572872 | tf_op jit(solution)/shard_map/ppermute | solution.py:294
  3.6 9.9 %collective-permute-start.1 = (bf16[64,16,128]{2,1,0:T(8,128)(2,1)S(1)}, bf16[64,16,128]{2,1,0:T(8,128)(2,1)S(1)}, u32[]{:S(2)}, u32[]{:S(2)}) collective-permute-start(bf16[64,16,128]{2,1,0:T(8,128)(2,1)S(1)} %fusion.after_hbm), channel_id=1, source_target_pairs={{0,2},{1,3},{2,0},{3,1},{4,6},{5,7},{6,4},{7,5},{8,10},{9,11},{10,... | collective-permute-start | bytes 786440 | tf_op jit(solution)/shard_map/ppermute | solution.py:294
  9.1 34.9 %collective-permute-start.5 = (bf16[2,1216,256]{2,1,0:T(8,128)(2,1)S(1)}, bf16[2,1216,256]{2,1,0:T(8,128)(2,1)S(1)}, u32[]{:S(2)}, u32[]{:S(2)}) collective-permute-start(bf16[2,1216,256]{2,1,0:T(8,128)(2,1)S(1)} %get-tuple-element.13.refs_1_.refs_2_.refs_4_), channel_id=1, source_target_pairs={{0,192},{4,196},{8,200},{12,204},{16,208},{20,212},{24,216},{28,22... | collective-permute-start | bytes 3735560 | tf_op jit(solution)/shard_map/ppermute | solution.py:341
  35.6 7.9 %collective-permute-start.3 = (bf16[32,2,16,128]{3,2,1,0:T(8,128)(2,1)S(1)}, bf16[32,2,16,128]{3,2,1,0:T(8,128)(2,1)S(1)}, u32[]{:S(2)}, u32[]{:S(2)}) collective-permute-start(bf16[32,2,16,128]{3,2,1,0:T(8,128)(2,1)S(1)} %all_to_all.10.refs_0_), channel_id=1, source_target_pairs={{0,2},{1,3},{2,0},{3,1},{4,6},{5,7},{6,4},{7,5},{8,10},{9,11},{10,... | collective-permute-start | bytes 786440 | tf_op jit(solution)/shard_map/ppermute | solution.py:294
  36.3 7.1 %collective-permute-start.2 = (bf16[32,2,16,128]{3,2,1,0:T(8,128)(2,1)S(1)}, bf16[32,2,16,128]{3,2,1,0:T(8,128)(2,1)S(1)}, u32[]{:S(2)}, u32[]{:S(2)}) collective-permute-start(bf16[32,2,16,128]{3,2,1,0:T(8,128)(2,1)S(1)} %all_to_all.10.refs_0_), channel_id=1, source_target_pairs={{0,1},{1,0},{2,3},{3,2},{4,5},{5,4},{6,7},{7,6},{8,9},{9,8},{10,11... | collective-permute-start | bytes 786440 | tf_op jit(solution)/shard_map/ppermute | solution.py:294
  43.4 1.5 %collective-permute-start.4 = (bf16[32,2,16,128]{3,2,1,0:T(8,128)(2,1)S(1)}, bf16[32,2,16,128]{3,2,1,0:T(8,128)(2,1)S(1)}, u32[]{:S(2)}, u32[]{:S(2)}) collective-permute-start(bf16[32,2,16,128]{3,2,1,0:T(8,128)(2,1)S(1)} %collective-permute-done.3.refs_1_.refs_2_), channel_id=1, source_target_pairs={{0,1},{1,0},{2,3},{3,2},{4,5},{5,4},{6,7},{7,6},{8,9},{9,8},{10,11... | collective-permute-start | bytes 786440 | tf_op jit(solution)/shard_map/ppermute | solution.py:294
  46.1 5.6 %copy-start.2 = (f32[1200]{0:T(1024)S(1)}, f32[1200]{0:T(1024)}, u32[]{:S(2)}) copy-start(f32[1200]{0:T(1024)} %vir_e_ref.1) | copy-start | bytes 14404
  46.1 5.6 %copy-start = (s32[1200]{0:T(1024)S(1)}, s32[1200]{0:T(1024)}, u32[]{:S(2)}) copy-start(s32[1200]{0:T(1024)} %vir_ref.1) | copy-start | bytes 14404
  46.1 5.6 %copy-start.1 = (f32[16,1200]{1,0:T(8,128)S(1)}, f32[16,1200]{1,0:T(8,128)}, u32[]{:S(2)}) copy-start(f32[16,1200]{1,0:T(8,128)} %res_ref.1) | copy-start | bytes 230404
  46.1 5.6 %copy-start.3 = (s32[128]{0:T(128)S(1)}, s32[128]{0:T(128)}, u32[]{:S(2)}) copy-start(s32[128]{0:T(128)} %occ_ref.1) | copy-start | bytes 1540
  46.1 5.6 %copy-start.4 = (f32[128]{0:T(128)S(1)}, f32[128]{0:T(128)}, u32[]{:S(2)}) copy-start(f32[128]{0:T(128)} %occ_e_ref.1) | copy-start | bytes 1540
  46.9 16.4 %all-to-all-start.1 = ((f16[32,16,256]{2,1,0:T(8,128)(2,1)}), f16[32,16,256]{2,1,0:T(8,128)(2,1)S(1)}, u32[]{:S(2)}, u32[]{:S(2)}) async-start(f16[32,16,256]{2,1,0:T(8,128)(2,1)} %bitcast.3), calls=%async_computation.1 | async-start | bytes 524288 | tf_op jit(solution)/shard_map/all_to_all | solution.py:361

commit v6 on v5

--- a/solution.py
+++ b/solution.py
@@ -31,7 +31,45 @@
     return shift
 
 
-def fold_amplitudes(odd, amp_hbm, occ_vec_hbm, occ_hbm, vir_hbm, after_hbm, out_ref, amp_ref, occ_vec_ref, occ_ref, vir_ref, mask_ref, sems):
+def label_tables(occ_ref, vir_ref, lab_ref, vec_ref, tab_ref):
+    v = vir_ref.shape[0]
+    begins = []
+    for label in range(1, 8):
+        lo, hi = jnp.int32(0), jnp.int32(v)
+        for _ in range(v.bit_length()):
+            mid = jnp.minimum((lo + hi) // 2, v - 1)
+            reached = vir_ref[mid] >= label
+            lo, hi = jnp.where(reached, lo, mid + 1), jnp.where(reached, mid, hi)
+        begins.append(hi)
+
+    def labels_of(orbital):
+        return sum((orbital >= begin).astype(jnp.int32) for begin in begins)
+
+    for c in range(0, v, 80):
+        at = lax.broadcasted_iota(jnp.int32, (80, 128), 0) + c
+        lab_ref[c : c + 80, :] = labels_of(at).astype(jnp.bfloat16)
+    vir_vec = labels_of(lax.broadcasted_iota(jnp.int32, (1, v), 1))
+    row = lax.axis_index("row")
+    for k in range(2):
+        vec_ref[k] = vir_vec ^ (occ_ref[2 * row + k] ^ occ_ref[1 + lax.axis_index("col")])
+    high = lax.broadcasted_iota(jnp.int32, (1, 2 * QUARTER), 1) >= QUARTER
+    wanted = []
+    for partner in PARTNERS:
+        other = 2 * (row ^ partner)
+        wanted.append(jnp.where(high, occ_ref[other + 1], occ_ref[other]) ^ occ_ref[0])
+    for block in range(tab_ref.shape[1]):
+        size = min(QUARTER, v - block * QUARTER)
+        x = jnp.full((1, QUARTER), 64, jnp.int32)
+        if size > 0:
+            x = vir_vec[:, block * QUARTER : block * QUARTER + size]
+            if size < QUARTER:
+                x = jnp.concatenate([x, jnp.full((1, QUARTER - size), 64, jnp.int32)], axis=1)
+        for d in range(FAR):
+            tab_ref[d, block : block + 1, :] = jnp.concatenate([x, x], axis=1) ^ wanted[d]
+
+
+def fold_amplitudes(odd, amp_hbm, occ_vec_hbm, occ_hbm, vir_hbm, after_hbm, out_ref, *refs):
+    tables, (amp_ref, occ_vec_ref, occ_ref, vir_ref, mask_ref, sems) = refs[:-6], refs[-6:]
     cols, rows, occ = amp_ref.shape
     step = cols // (sems.shape[0] - 3)
     small = [
@@ -53,6 +91,8 @@
     a_labels = jnp.zeros((rows, occ), jnp.int32)
     for a in range(rows):
         a_labels = jnp.where(row_id == a, vir_ref[first_a + a], a_labels)
+    if tables:
+        label_tables(occ_ref, vir_ref, *tables)
     wanted = occ_ref[0] ^ occ_vec_ref[...] ^ a_labels
     for label in range(8):
         mask_ref[label] = jnp.where(wanted == label, 1.0, 0.0).astype(jnp.bfloat16)
@@ -117,9 +157,8 @@
             out_ref[i, d] = turned_ref[pl.ds(pl.multiple_of(row * rows, rows), rows), :].astype(jnp.bfloat16)
 
 
-def fold_integrals(int_hbm, occ_hbm, vir_hbm, after_hbm, out_ref, lab_ref, vec_ref, tab_ref, int_ref, occ_ref, vir_ref, small, sems):
+def fold_integrals(int_hbm, lab_ref, vec_ref, after_hbm, out_ref, int_ref, sems):
     _, v, width = int_ref.shape
-    near = [pltpu.make_async_copy(vir_hbm, vir_ref, small.at[0]), pltpu.make_async_copy(occ_hbm, occ_ref, small.at[1])]
     step = v // sems.shape[1]
     copies = [
         [
@@ -128,44 +167,10 @@
         ]
         for k in range(2)
     ]
-    for copy in near + copies[0] + copies[1]:
+    for copy in copies[0] + copies[1]:
         copy.start()
-    for copy in near:
-        copy.wait()
-    begins = []
-    for label in range(1, 8):
-        lo, hi = jnp.int32(0), jnp.int32(v)
-        for _ in range(v.bit_length()):
-            mid = jnp.minimum((lo + hi) // 2, v - 1)
-            reached = vir_ref[mid] >= label
-            lo, hi = jnp.where(reached, lo, mid + 1), jnp.where(reached, mid, hi)
-        begins.append(hi)
-
-    def labels_of(orbital):
-        return sum((orbital >= begin).astype(jnp.int32) for begin in begins)
-
-    for c in range(0, v, 80):
-        at = lax.broadcasted_iota(jnp.int32, (80, 128), 0) + c
-        lab_ref[c : c + 80, :] = labels_of(at).astype(jnp.bfloat16)
-    vir_vec = labels_of(lax.broadcasted_iota(jnp.int32, (1, width), 1))
-    vec_ref[...] = vir_vec
-    high = lax.broadcasted_iota(jnp.int32, (1, 2 * QUARTER), 1) >= QUARTER
-    wanted = []
-    for partner in PARTNERS:
-        other = 2 * (lax.axis_index("row") ^ partner)
-        wanted.append(jnp.where(high, occ_ref[other + 1], occ_ref[other]) ^ occ_ref[0])
-    for block in range(tab_ref.shape[1]):
-        size = min(QUARTER, v - block * QUARTER)
-        x = jnp.full((1, QUARTER), 64, jnp.int32)
-        if size > 0:
-            x = vir_vec[:, block * QUARTER : block * QUARTER + size]
-            if size < QUARTER:
-                x = jnp.concatenate([x, jnp.full((1, QUARTER - size), 64, jnp.int32)], axis=1)
-        for d in range(FAR):
-            tab_ref[d, block : block + 1, :] = jnp.concatenate([x, x], axis=1) ^ wanted[d]
     for k in range(2):
-        label = occ_ref[lax.axis_index("row") * 2 + k] ^ occ_ref[1 + lax.axis_index("col")]
-        b_labels = (vir_vec ^ label).astype(jnp.bfloat16)
+        b_labels = vec_ref[k].astype(jnp.bfloat16)
         for i, copy in enumerate(copies[k]):
             copy.wait()
             for c in range(i * step, (i + 1) * step, 80):
@@ -225,7 +230,7 @@
     for a in range(rows):
         a_labels = jnp.where(row_id == a, vir_ref[first_a + a], a_labels)
         a_energy = jnp.where(row_id == a, vir_e_ref[first_a + a], a_energy)
-    b_labels = vir_vec_ref[...] ^ occ_ref[0] ^ occ_ref[j]
+    b_labels = vir_vec_ref[0] ^ occ_ref[2 * lax.axis_index("row")] ^ occ_ref[0]
     for b in range(0, v, 128):
         width = min(128, v - b)
         at = slice(b, b + width)
@@ -263,12 +268,12 @@
     occ_vec = occupied_irrep.reshape(1, o_win)
 
     chunks = 6
-    def folded(odd, after):
+    def folded(odd, after, tables):
         return pl.pallas_call(
             functools.partial(fold_amplitudes, odd),
-            out_shape=jax.ShapeDtypeStruct((2, QUARTER, rows, o_win), jnp.bfloat16),
+            out_shape=[jax.ShapeDtypeStruct((2, QUARTER, rows, o_win), jnp.bfloat16)] + tables,
             in_specs=[hbm] * 5,
-            out_specs=vmem,
+            out_specs=[vmem] * (1 + len(tables)),
             scratch_shapes=[
                 pltpu.VMEM((cols, rows, o_win), jnp.bfloat16),
                 pltpu.VMEM((1, o_win), jnp.int32),
@@ -287,39 +292,31 @@
             after,
         )
 
-    send = folded(1, pltpu.with_memory_space_constraint(occupied_irrep, pltpu.HBM))
-    keep = folded(0, send)
+    (send,) = folded(1, pltpu.with_memory_space_constraint(occupied_irrep, pltpu.HBM), [])
+    tables = [
+        jax.ShapeDtypeStruct((v, 128), jnp.bfloat16),
+        jax.ShapeDtypeStruct((occ_local, 1, v), jnp.int32),
+        jax.ShapeDtypeStruct((FAR, 4 * (-(-v // FOLD)), 2 * QUARTER), jnp.int32),
+    ]
+    keep, labels, vir_vecs, table = folded(0, send, tables)
 
     def swap(x, p):
         return lax.ppermute(x, "col", [(m, m ^ p) for m in range(4)])
 
     got = swap(send, 1)
     passed = keep[1] + got[1]
-    w, labels, vir_vec, table = pl.pallas_call(
+    w = pl.pallas_call(
         fold_integrals,
-        out_shape=[
-            jax.ShapeDtypeStruct((occ_local, -(-v // QUARTER) * QUARTER, FOLD), jnp.bfloat16),
-            jax.ShapeDtypeStruct((v, 128), jnp.bfloat16),
-            jax.ShapeDtypeStruct((1, v), jnp.int32),
-            jax.ShapeDtypeStruct((FAR, 4 * (-(-v // FOLD)), 2 * QUARTER), jnp.int32),
-        ],
-        in_specs=[hbm] * 4,
-        out_specs=[vmem] * 4,
+        out_shape=jax.ShapeDtypeStruct((occ_local, -(-v // QUARTER) * QUARTER, FOLD), jnp.bfloat16),
+        in_specs=[hbm, vmem, vmem, hbm],
+        out_specs=vmem,
         scratch_shapes=[
             pltpu.VMEM((occ_local, v, n_local), jnp.bfloat16),
-            pltpu.SMEM((o_win,), jnp.int32),
-            pltpu.SMEM((v,), jnp.int32),
-            pltpu.SemaphoreType.DMA((2,)),
             pltpu.SemaphoreType.DMA((occ_local, 5)),
         ],
         compiler_params=big,
         name="fold_integrals",
-    )(
-        pltpu.with_memory_space_constraint(integrals, pltpu.HBM),
-        pltpu.with_memory_space_constraint(occupied_irrep, pltpu.HBM),
-        pltpu.with_memory_space_constraint(virtual_irrep, pltpu.HBM),
-        passed,
-    )
+    )(pltpu.with_memory_space_constraint(integrals, pltpu.HBM), labels, vir_vecs, passed)
     far = swap(passed, 2)
     turned = pl.pallas_call(
         turn_amplitudes,
@@ -375,7 +372,7 @@
         name="prepare",
     )(
         residual_in,
-        vir_vec,
+        vir_vecs,
         virtual_energy.reshape(1, v),
         occupied_irrep,
         virtual_irrep,

time: 64.5 us -> 65.5 us (1.016)
  transfers between devices with their start and end apart: 7 -> 7, of which waited for: 5 -> 4; matrix products, arithmetic and copies ran while one was open for 0% -> 0% of each run, Pallas kernels for 11% -> 11%
where the time goes in v6:
time: 65.5 us; the launch traced here: 65 us
  waiting for transfers between devices  22 us (34%)
  blocking collectives  21.7 us (33%)
  Pallas kernels  10.6 us (16%)
  starting transfers between devices  9.52 us (15%)
  other arithmetic  0.83 us (1%)
    all_to_all x1, blocking collectives, local(): lax.all_to_all(turned, 'row', split_axis=0, concat_axis=0, tiled=True, ax...  21.7 us
    ppermute x5, waiting for transfers between devices, swap(): return lax.ppermute(x, 'col', [(m, m ^ p) for m in range(4)])  11.3 us
    all_to_all x1, waiting for transfers between devices, local(): lax.all_to_all(partial.astype(SEND_TYPE).reshape(near, rows, FOLD), 'row'...  10.7 us
    all_to_all x1, starting transfers between devices, local(): lax.all_to_all(partial.astype(SEND_TYPE).reshape(near, rows, FOLD), 'row'...  4.91 us
    pallas_call x2, Pallas kernels, folded(): pl.pallas_call(functools.partial(fold_amplitudes, odd), out_shape=[jax.Sh...  3.69 us
    ppermute x5, starting transfers between devices, swap(): return lax.ppermute(x, 'col', [(m, m ^ p) for m in range(4)])  3.25 us
    pallas_call x1, Pallas kernels, local(): pl.pallas_call(fold_integrals, out_shape=jax.ShapeDtypeStruct((occ_local,...  2.95 us
    pallas_call x3, Pallas kernels, contracted(): pl.pallas_call(functools.partial(contract, terms, last), out_shape=jax.Sh...  1.98 us
  transfers between devices with their start and end apart: 7, of which 4 were waited for; matrix products, arithmetic and copies ran while one was open for 0% of the time, Pallas kernels for 11%

profile of v6, /device:TPU:4, one launch (start us, length us, event | category | flops | bytes accessed | tf_op | source)
XLA Modules:
  0.0 65.0 jit_solution(9414225082824611584)
XLA Ops:
  0.0 1.5 %fold_amplitudes.2.after_hbm = bf16[2,64,16,128]{3,2,1,0:T(8,128)(2,1)S(1)} custom-call(bf16[300,16,128]{2,1,0:T(8,128)(2,1)} %bitcast.7, s32[1,128]{1,0:T(1,128)} %bitcast.5, s32[128]{0:T(128)} %occ_ref.1, s32[1200]{0:T(1024)} %vir_ref.1, s32[128]{0:T(128)} %occ_ref.1), custom_call_target="tpu_custom_call" | custom-call | tf_op jit(solution)/shard_map/fold_amplitudes/pallas_call | solution.py:272
  1.5 0.1 collective-permute-start
  1.6 2.1 %fold_amplitudes.3 = (bf16[2,64,16,128]{3,2,1,0:T(8,128)(2,1)S(1)}, bf16[1200,128]{1,0:T(8,128)(2,1)S(1)}, s32[2,1,1200]{2,1,0:T(1,128)S(1)}, s32[2,20,128]{2,1,0:T(8,128)S(1)}) custom-call(bf16[300,16,128]{2,1,0:T(8,128)(2,1)} %bitcast.8, s32[1,128]{1,0:T(1,128)} %bitcast.6, s32[128]{0:T(128)} %occ_ref.1, s32[1200]{0:T(1024)} %vir_ref.1, ...), custom_call_target="tpu_custom_call" | custom-call | tf_op jit(solution)/shard_map/fold_amplitudes/pallas_call | solution.py:272
  3.8 0.0 collective-permute-done.b_ref
  3.9 2.4 %collective-permute-start.1 = (bf16[64,16,128]{2,1,0:T(8,128)(2,1)S(1)}, bf16[64,16,128]{2,1,0:T(8,128)(2,1)S(1)}, u32[]{:S(2)}, u32[]{:S(2)}) collective-permute-start(bf16[64,16,128]{2,1,0:T(8,128)(2,1)S(1)} %fusion.after_hbm), channel_id=1, source_target_pairs={{0,2},{1,3},{2,0},{3,1},{4,6},{5,7},{6,4},{7,5},{8,10},{9,11},{10,... | collective-permute-start | bytes 786440 | tf_op jit(solution)/shard_map/ppermute | solution.py:304
  6.2 2.9 %fold_integrals.1.refs_1_.refs_2_.refs_4_ = bf16[2,1216,256]{2,1,0:T(8,128)(2,1)S(1)} custom-call(bf16[2,1200,1200]{2,1,0:T(8,128)(2,1)} %int_hbm.1, bf16[1200,128]{1,0:T(8,128)(2,1)S(1)} %get-tuple-element.14.lab_ref.refs_2_.refs_3_.refs_6_, s32[2,1,1200]{2,1,0:T(1,128)S(1)} %get-tuple-element.15.vec_ref.vir_vec_ref, bf16[64,16,128]{2,1,0:T(8,128)(2,1)S(1)} %fusion.after_hbm), custom_call_target="tpu_custom_call" | custom-call | tf_op jit(solution)/shard_map/fold_integrals/pallas_call | solution.py:308
  9.2 1.4 %collective-permute-start.5 = (bf16[2,1216,256]{2,1,0:T(8,128)(2,1)S(1)}, bf16[2,1216,256]{2,1,0:T(8,128)(2,1)S(1)}, u32[]{:S(2)}, u32[]{:S(2)}) collective-permute-start(bf16[2,1216,256]{2,1,0:T(8,128)(2,1)S(1)} %fold_integrals.1.refs_1_.refs_2_.refs_4_), channel_id=1, source_target_pairs={{0,192},{4,196},{8,200},{12,204},{16,208},{20,212},{24,216},{28,22... | collective-permute-start | bytes 3735560 | tf_op jit(solution)/shard_map/ppermute | solution.py:338
  10.5 3.6 %collective-permute-done.1.c_ref = bf16[64,16,128]{2,1,0:T(8,128)(2,1)S(1)} collective-permute-done((bf16[64,16,128]{2,1,0:T(8,128)(2,1)S(1)}, bf16[64,16,128]{2,1,0:T(8,128)(2,1)S(1)}, u32[]{:S(2)}, u32[]{:S(2)}) %collective-permute-start.1) | collective-permute-done | bytes 262176 | tf_op jit(solution)/shard_map/ppermute | solution.py:304
  14.1 0.6 turn_amplitudes.1
  14.8 21.7 %all_to_all.10.refs_0_ = bf16[32,2,16,128]{3,2,1,0:T(8,128)(2,1)S(1)} all-to-all(bf16[32,2,16,128]{3,2,1,0:T(8,128)(2,1)S(1)} %turn_amplitudes.1), channel_id=1, replica_groups={{0,4,8,12,16,20,24,28,32,36,40,44,48,52,56,60,64,68,72,76,80,84,88,92,9..., dimensions={0} | all-to-all | bytes 524288 | tf_op jit(solution)/shard_map/all_to_all | solution.py:335
  36.5 0.8 %collective-permute-start.3 = (bf16[32,2,16,128]{3,2,1,0:T(8,128)(2,1)S(1)}, bf16[32,2,16,128]{3,2,1,0:T(8,128)(2,1)S(1)}, u32[]{:S(2)}, u32[]{:S(2)}) collective-permute-start(bf16[32,2,16,128]{3,2,1,0:T(8,128)(2,1)S(1)} %all_to_all.10.refs_0_), channel_id=1, source_target_pairs={{0,2},{1,3},{2,0},{3,1},{4,6},{5,7},{6,4},{7,5},{8,10},{9,11},{10,... | collective-permute-start | bytes 786440 | tf_op jit(solution)/shard_map/ppermute | solution.py:304
  37.3 0.0 collective-permute-start.2
  37.3 0.4 contract.3.refs_5_
  37.6 6.7 %collective-permute-done.3.refs_1_.refs_2_ = bf16[32,2,16,128]{3,2,1,0:T(8,128)(2,1)S(1)} collective-permute-done((bf16[32,2,16,128]{3,2,1,0:T(8,128)(2,1)S(1)}, bf16[32,2,16,128]{3,2,1,0:T(8,128)(2,1)S(1)}, u32[]{:S(2)}, u32[]{:S(2)}) %collective-permute-start.3) | collective-permute-done | bytes 262176 | tf_op jit(solution)/shard_map/ppermute | solution.py:304
  44.4 0.0 collective-permute-start.4
  44.4 0.0 collective-permute-done.2.refs_0_.refs_1_
  44.4 0.5 contract.4.refs_8_
  44.9 0.0 collective-permute-done.5.refs_5_
  44.9 1.0 %collective-permute-done.4.refs_3_ = bf16[32,2,16,128]{3,2,1,0:T(8,128)(2,1)S(1)} collective-permute-done((bf16[32,2,16,128]{3,2,1,0:T(8,128)(2,1)S(1)}, bf16[32,2,16,128]{3,2,1,0:T(8,128)(2,1)S(1)}, u32[]{:S(2)}, u32[]{:S(2)}) %collective-permute-start.4) | collective-permute-done | bytes 262176 | tf_op jit(solution)/shard_map/ppermute | solution.py:304
  45.9 1.1 %contract.5 = f32[512,256]{1,0:T(8,128)S(1)} custom-call(bf16[32,2,16,128]{3,2,1,0:T(8,128)(2,1)S(1)} %all_to_all.10.refs_0_, bf16[32,2,16,128]{3,2,1,0:T(8,128)(2,1)S(1)} %collective-permute-done.2.refs_0_.refs_1_, bf16[32,2,16,128]{3,2,1,0:T(8,128)(2,1)S(1)} %collective-permute-done.3.refs_1_.refs_2_, ...), custom_call_target="tpu_custom_call" | custom-call | tf_op jit(solution)/shard_map/contract/pallas_call | solution.py:343
  47.0 0.0 copy-start.2
  47.0 0.0 copy-start
  47.0 0.0 copy-start.1
  47.0 0.0 copy-start.3
  47.0 0.0 copy-start.4
  47.0 0.7 %convert_element_type.6 = f16[512,256]{1,0:T(8,128)(2,1)} convert(f32[512,256]{1,0:T(8,128)S(1)} %contract.5) | non-fusion elementwise | flops 131072 | bytes 786432 | tf_op jit(solution)/shard_map/convert_element_type | solution.py:359
  47.8 4.9 %all-to-all-start.1 = ((f16[32,16,256]{2,1,0:T(8,128)(2,1)}), f16[32,16,256]{2,1,0:T(8,128)(2,1)S(1)}, u32[]{:S(2)}, u32[]{:S(2)}) async-start(f16[32,16,256]{2,1,0:T(8,128)(2,1)} %bitcast.3), calls=%async_computation.1 | async-start | bytes 524288 | tf_op jit(solution)/shard_map/all_to_all | solution.py:358
  52.7 0.0 copy-done
  52.7 0.0 copy-done.1
  52.8 0.8 %prepare.1 = (f32[16,1200]{1,0:T(8,128)S(1)}, f32[16,1200]{1,0:T(8,128)S(1)}) custom-call(f32[16,1200]{1,0:T(8,128)S(1)} %copy-done, s32[2,1,1200]{2,1,0:T(1,128)S(1)} %get-tuple-element.15.vec_ref.vir_vec_ref, f32[1,1200]{1,0:T(1,128)S(1)} %reshape.12.energy_vec_ref, s32[128]{0:T(128)S(1)} %copy-done.3, s32[1200]{0:T(1024)S(1)} %copy-done.1, ...), custom_call_target="tpu_custom_call" | custom-call | tf_op jit(solution)/shard_map/prepare/pallas_call | solution.py:366
  53.5 10.7 %all-to-all-done.1 = f16[32,16,256]{2,1,0:T(8,128)(2,1)S(1)} async-done(((f16[32,16,256]{2,1,0:T(8,128)(2,1)}), f16[32,16,256]{2,1,0:T(8,128)(2,1)S(1)}, u32[]{:S(2)}, u32[]{:S(2)}) %all-to-all-start.1) | async-done | bytes 262176 | tf_op jit(solution)/shard_map/all_to_all | solution.py:358
  64.3 0.6 finish.1
  (6 shorter events, 0.1 us)
Async XLA Ops:
  1.5 2.3 %collective-permute-start = (bf16[2,64,16,128]{3,2,1,0:T(8,128)(2,1)S(1)}, bf16[2,64,16,128]{3,2,1,0:T(8,128)(2,1)S(1)}, u32[]{:S(2)}, u32[]{:S(2)}) collective-permute-start(bf16[2,64,16,128]{3,2,1,0:T(8,128)(2,1)S(1)} %fold_amplitudes.2.after_hbm), channel_id=1, source_target_pairs={{0,1},{1,0},{2,3},{3,2},{4,5},{5,4},{6,7},{7,6},{8,9},{9,8},{10,11... | collective-permute-start | bytes 1572872 | tf_op jit(solution)/shard_map/ppermute | solution.py:304
  3.9 10.3 %collective-permute-start.1 = (bf16[64,16,128]{2,1,0:T(8,128)(2,1)S(1)}, bf16[64,16,128]{2,1,0:T(8,128)(2,1)S(1)}, u32[]{:S(2)}, u32[]{:S(2)}) collective-permute-start(bf16[64,16,128]{2,1,0:T(8,128)(2,1)S(1)} %fusion.after_hbm), channel_id=1, source_target_pairs={{0,2},{1,3},{2,0},{3,1},{4,6},{5,7},{6,4},{7,5},{8,10},{9,11},{10,... | collective-permute-start | bytes 786440 | tf_op jit(solution)/shard_map/ppermute | solution.py:304
  9.2 35.7 %collective-permute-start.5 = (bf16[2,1216,256]{2,1,0:T(8,128)(2,1)S(1)}, bf16[2,1216,256]{2,1,0:T(8,128)(2,1)S(1)}, u32[]{:S(2)}, u32[]{:S(2)}) collective-permute-start(bf16[2,1216,256]{2,1,0:T(8,128)(2,1)S(1)} %fold_integrals.1.refs_1_.refs_2_.refs_4_), channel_id=1, source_target_pairs={{0,192},{4,196},{8,200},{12,204},{16,208},{20,212},{24,216},{28,22... | collective-permute-start | bytes 3735560 | tf_op jit(solution)/shard_map/ppermute | solution.py:338
  36.5 7.9 %collective-permute-start.3 = (bf16[32,2,16,128]{3,2,1,0:T(8,128)(2,1)S(1)}, bf16[32,2,16,128]{3,2,1,0:T(8,128)(2,1)S(1)}, u32[]{:S(2)}, u32[]{:S(2)}) collective-permute-start(bf16[32,2,16,128]{3,2,1,0:T(8,128)(2,1)S(1)} %all_to_all.10.refs_0_), channel_id=1, source_target_pairs={{0,2},{1,3},{2,0},{3,1},{4,6},{5,7},{6,4},{7,5},{8,10},{9,11},{10,... | collective-permute-start | bytes 786440 | tf_op jit(solution)/shard_map/ppermute | solution.py:304
  37.3 7.1 %collective-permute-start.2 = (bf16[32,2,16,128]{3,2,1,0:T(8,128)(2,1)S(1)}, bf16[32,2,16,128]{3,2,1,0:T(8,128)(2,1)S(1)}, u32[]{:S(2)}, u32[]{:S(2)}) collective-permute-start(bf16[32,2,16,128]{3,2,1,0:T(8,128)(2,1)S(1)} %all_to_all.10.refs_0_), channel_id=1, source_target_pairs={{0,1},{1,0},{2,3},{3,2},{4,5},{5,4},{6,7},{7,6},{8,9},{9,8},{10,11... | collective-permute-start | bytes 786440 | tf_op jit(solution)/shard_map/ppermute | solution.py:304
  44.4 1.5 %collective-permute-start.4 = (bf16[32,2,16,128]{3,2,1,0:T(8,128)(2,1)S(1)}, bf16[32,2,16,128]{3,2,1,0:T(8,128)(2,1)S(1)}, u32[]{:S(2)}, u32[]{:S(2)}) collective-permute-start(bf16[32,2,16,128]{3,2,1,0:T(8,128)(2,1)S(1)} %collective-permute-done.3.refs_1_.refs_2_), channel_id=1, source_target_pairs={{0,1},{1,0},{2,3},{3,2},{4,5},{5,4},{6,7},{7,6},{8,9},{9,8},{10,11... | collective-permute-start | bytes 786440 | tf_op jit(solution)/shard_map/ppermute | solution.py:304
  47.0 5.7 %copy-start.2 = (f32[1200]{0:T(1024)S(1)}, f32[1200]{0:T(1024)}, u32[]{:S(2)}) copy-start(f32[1200]{0:T(1024)} %vir_e_ref.1) | copy-start | bytes 14404
  47.0 5.7 %copy-start = (f32[16,1200]{1,0:T(8,128)S(1)}, f32[16,1200]{1,0:T(8,128)}, u32[]{:S(2)}) copy-start(f32[16,1200]{1,0:T(8,128)} %res_ref.1) | copy-start | bytes 230404
  47.0 5.7 %copy-start.1 = (s32[1200]{0:T(1024)S(1)}, s32[1200]{0:T(1024)}, u32[]{:S(2)}) copy-start(s32[1200]{0:T(1024)} %vir_ref.1) | copy-start | bytes 14404
  47.0 5.7 %copy-start.3 = (s32[128]{0:T(128)S(1)}, s32[128]{0:T(128)}, u32[]{:S(2)}) copy-start(s32[128]{0:T(128)} %occ_ref.1) | copy-start | bytes 1540
  47.0 5.7 %copy-start.4 = (f32[128]{0:T(128)S(1)}, f32[128]{0:T(128)}, u32[]{:S(2)}) copy-start(f32[128]{0:T(128)} %occ_e_ref.1) | copy-start | bytes 1540
  47.8 16.5 %all-to-all-start.1 = ((f16[32,16,256]{2,1,0:T(8,128)(2,1)}), f16[32,16,256]{2,1,0:T(8,128)(2,1)S(1)}, u32[]{:S(2)}, u32[]{:S(2)}) async-start(f16[32,16,256]{2,1,0:T(8,128)(2,1)} %bitcast.3), calls=%async_computation.1 | async-start | bytes 524288 | tf_op jit(solution)/shard_map/all_to_all | solution.py:358

commit v7 on v5

--- a/solution.py
+++ b/solution.py
@@ -160,7 +160,7 @@
         if size > 0:
             x = vir_vec[:, block * QUARTER : block * QUARTER + size]
             if size < QUARTER:
-                x = jnp.concatenate([x, jnp.full((1, QUARTER - size), 64, jnp.int32)], axis=1)
+                x = jnp.concatenate([jnp.full((1, QUARTER - size), 64, jnp.int32), x], axis=1)
         for d in range(FAR):
             tab_ref[d, block : block + 1, :] = jnp.concatenate([x, x], axis=1) ^ wanted[d]
     for k in range(2):
@@ -181,7 +181,6 @@
                             x = jnp.concatenate([x, jnp.zeros((80, 128 - size), x.dtype)], axis=1)
                         total = x if total is None else total + x
                     out_ref[k, rows, n * 128 : (n + 1) * 128] = total
-        out_ref[k, v:, :] = jnp.zeros((out_ref.shape[1] - v, FOLD), out_ref.dtype)
 
 
 def contract(terms, last, *refs):
@@ -205,6 +204,10 @@
         for p, d, t in blocks[n : n + 2]:
             block = 4 * t + (me ^ p)
             x = t_refs[quarters.index(p)][:, d].reshape(near * rows, lanes)
+            if 4 * t * QUARTER + FOLD > tall:
+                late = QUARTER - tall % QUARTER
+                moved = jnp.concatenate([x[:, lanes - late :], x[:, : lanes - late]], axis=1)
+                x = lax.select(block == tall // QUARTER, moved, x)
             c_labels = tab_ref[d, pl.ds(block, 1), :].astype(jnp.bfloat16)
             lhs.append(jnp.where(a_labels == c_labels, x, jnp.zeros_like(x)))
             c = pl.multiple_of(jnp.minimum(block * QUARTER, tall - QUARTER), QUARTER)
@@ -298,7 +301,7 @@
     w, labels, vir_vec, table = pl.pallas_call(
         fold_integrals,
         out_shape=[
-            jax.ShapeDtypeStruct((occ_local, -(-v // QUARTER) * QUARTER, FOLD), jnp.bfloat16),
+            jax.ShapeDtypeStruct((occ_local, v, FOLD), jnp.bfloat16),
             jax.ShapeDtypeStruct((v, 128), jnp.bfloat16),
             jax.ShapeDtypeStruct((1, v), jnp.int32),
             jax.ShapeDtypeStruct((FAR, 4 * (-(-v // FOLD)), 2 * QUARTER), jnp.int32),

time: 64.5 us -> 64.5 us (level)
  no operation moved by 1% of the time
where the time goes in v7:
time: 64.5 us; the launch traced here: 64 us
  waiting for transfers between devices  21.8 us (34%)
  blocking collectives  21.4 us (33%)
  Pallas kernels  10.3 us (16%)
  starting transfers between devices  9.34 us (14%)
  other arithmetic  0.82 us (1%)
    all_to_all x1, blocking collectives, local(): lax.all_to_all(turned, 'row', split_axis=0, concat_axis=0, tiled=True, ax...  21.4 us
    ppermute x5, waiting for transfers between devices, swap(): return lax.ppermute(x, 'col', [(m, m ^ p) for m in range(4)])  11.1 us
    all_to_all x1, waiting for transfers between devices, local(): lax.all_to_all(partial.astype(SEND_TYPE).reshape(near, rows, FOLD), 'row'...  10.7 us
    all_to_all x1, starting transfers between devices, local(): lax.all_to_all(partial.astype(SEND_TYPE).reshape(near, rows, FOLD), 'row'...  4.81 us
    pallas_call x1, Pallas kernels, local(): pl.pallas_call(fold_integrals, out_shape=[jax.ShapeDtypeStruct((occ_local...  3.27 us
    ppermute x5, starting transfers between devices, swap(): return lax.ppermute(x, 'col', [(m, m ^ p) for m in range(4)])  3.16 us
    pallas_call x2, Pallas kernels, folded(): pl.pallas_call(functools.partial(fold_amplitudes, odd), out_shape=jax.Sha...  3.02 us
    pallas_call x3, Pallas kernels, contracted(): pl.pallas_call(functools.partial(contract, terms, last), out_shape=jax.Sh...  2.03 us
  transfers between devices with their start and end apart: 7, of which 5 were waited for; matrix products, arithmetic and copies ran while one was open for 0% of the time, Pallas kernels for 11%

profile of v7, /device:TPU:4, one launch (start us, length us, event | category | flops | bytes accessed | tf_op | source)
XLA Modules:
  0.0 64.0 jit_solution(7059011224109058233)
XLA Ops:
  0.0 1.5 %fold_amplitudes.2.after_hbm = bf16[2,64,16,128]{3,2,1,0:T(8,128)(2,1)S(1)} custom-call(bf16[300,16,128]{2,1,0:T(8,128)(2,1)} %bitcast.7, s32[1,128]{1,0:T(1,128)} %bitcast.5, s32[128]{0:T(128)} %occ_ref.1, s32[1200]{0:T(1024)} %vir_ref.1, s32[128]{0:T(128)} %occ_ref.1), custom_call_target="tpu_custom_call" | custom-call | tf_op jit(solution)/shard_map/fold_amplitudes/pallas_call | solution.py:270
  1.5 0.1 collective-permute-start
  1.6 1.5 %fold_amplitudes.3.a_ref = bf16[2,64,16,128]{3,2,1,0:T(8,128)(2,1)S(1)} custom-call(bf16[300,16,128]{2,1,0:T(8,128)(2,1)} %bitcast.8, s32[1,128]{1,0:T(1,128)} %bitcast.6, s32[128]{0:T(128)} %occ_ref.1, s32[1200]{0:T(1024)} %vir_ref.1, bf16[2,64,16,128]{3,2,1,0:T(8,128)(2,1)S(1)} %fold_amplitudes.2.after_hbm), custom_call_target="tpu_custom_call" | custom-call | tf_op jit(solution)/shard_map/fold_amplitudes/pallas_call | solution.py:270
  3.1 0.4 collective-permute-done.b_ref
  3.6 2.3 %collective-permute-start.1 = (bf16[64,16,128]{2,1,0:T(8,128)(2,1)S(1)}, bf16[64,16,128]{2,1,0:T(8,128)(2,1)S(1)}, u32[]{:S(2)}, u32[]{:S(2)}) collective-permute-start(bf16[64,16,128]{2,1,0:T(8,128)(2,1)S(1)} %fusion.after_hbm), channel_id=1, source_target_pairs={{0,2},{1,3},{2,0},{3,1},{4,6},{5,7},{6,4},{7,5},{8,10},{9,11},{10,... | collective-permute-start | bytes 786440 | tf_op jit(solution)/shard_map/ppermute | solution.py:297
  5.9 3.3 %fold_integrals.1 = (bf16[2,1200,256]{2,1,0:T(8,128)(2,1)S(1)}, bf16[1200,128]{1,0:T(8,128)(2,1)S(1)}, s32[1,1200]{1,0:T(1,128)S(1)}, s32[2,20,128]{2,1,0:T(8,128)S(1)}) custom-call(bf16[2,1200,1200]{2,1,0:T(8,128)(2,1)} %int_hbm.1, s32[128]{0:T(128)} %occ_ref.1, s32[1200]{0:T(1024)} %vir_ref.1, bf16[64,16,128]{2,1,0:T(8,128)(2,1)S(1)} %fusion.after_hbm), custom_call_target="tpu_custom_call" | custom-call | tf_op jit(solution)/shard_map/fold_integrals/pallas_call | solution.py:301
  9.1 1.4 %collective-permute-start.5 = (bf16[2,1200,256]{2,1,0:T(8,128)(2,1)S(1)}, bf16[2,1200,256]{2,1,0:T(8,128)(2,1)S(1)}, u32[]{:S(2)}, u32[]{:S(2)}) collective-permute-start(bf16[2,1200,256]{2,1,0:T(8,128)(2,1)S(1)} %get-tuple-element.13.refs_1_.refs_2_.refs_4_), channel_id=1, source_target_pairs={{0,192},{4,196},{8,200},{12,204},{16,208},{20,212},{24,216},{28,22... | collective-permute-start | bytes 3686408 | tf_op jit(solution)/shard_map/ppermute | solution.py:344
  10.5 3.0 %collective-permute-done.1.c_ref = bf16[64,16,128]{2,1,0:T(8,128)(2,1)S(1)} collective-permute-done((bf16[64,16,128]{2,1,0:T(8,128)(2,1)S(1)}, bf16[64,16,128]{2,1,0:T(8,128)(2,1)S(1)}, u32[]{:S(2)}, u32[]{:S(2)}) %collective-permute-start.1) | collective-permute-done | bytes 262176 | tf_op jit(solution)/shard_map/ppermute | solution.py:297
  13.5 0.6 turn_amplitudes.1
  14.1 21.4 %all_to_all.10.refs_0_ = bf16[32,2,16,128]{3,2,1,0:T(8,128)(2,1)S(1)} all-to-all(bf16[32,2,16,128]{3,2,1,0:T(8,128)(2,1)S(1)} %turn_amplitudes.1), channel_id=1, replica_groups={{0,4,8,12,16,20,24,28,32,36,40,44,48,52,56,60,64,68,72,76,80,84,88,92,9..., dimensions={0} | all-to-all | bytes 524288 | tf_op jit(solution)/shard_map/all_to_all | solution.py:341
  35.5 0.8 %collective-permute-start.3 = (bf16[32,2,16,128]{3,2,1,0:T(8,128)(2,1)S(1)}, bf16[32,2,16,128]{3,2,1,0:T(8,128)(2,1)S(1)}, u32[]{:S(2)}, u32[]{:S(2)}) collective-permute-start(bf16[32,2,16,128]{3,2,1,0:T(8,128)(2,1)S(1)} %all_to_all.10.refs_0_), channel_id=1, source_target_pairs={{0,2},{1,3},{2,0},{3,1},{4,6},{5,7},{6,4},{7,5},{8,10},{9,11},{10,... | collective-permute-start | bytes 786440 | tf_op jit(solution)/shard_map/ppermute | solution.py:297
  36.3 0.0 collective-permute-start.2
  36.3 0.4 contract.3.refs_5_
  36.7 6.7 %collective-permute-done.3.refs_1_.refs_2_ = bf16[32,2,16,128]{3,2,1,0:T(8,128)(2,1)S(1)} collective-permute-done((bf16[32,2,16,128]{3,2,1,0:T(8,128)(2,1)S(1)}, bf16[32,2,16,128]{3,2,1,0:T(8,128)(2,1)S(1)}, u32[]{:S(2)}, u32[]{:S(2)}) %collective-permute-start.3) | collective-permute-done | bytes 262176 | tf_op jit(solution)/shard_map/ppermute | solution.py:297
  43.4 0.0 collective-permute-start.4
  43.4 0.0 collective-permute-done.2.refs_0_.refs_1_
  43.4 0.5 contract.4.refs_8_
  44.0 0.0 collective-permute-done.5.refs_5_
  44.0 1.0 %collective-permute-done.4.refs_3_ = bf16[32,2,16,128]{3,2,1,0:T(8,128)(2,1)S(1)} collective-permute-done((bf16[32,2,16,128]{3,2,1,0:T(8,128)(2,1)S(1)}, bf16[32,2,16,128]{3,2,1,0:T(8,128)(2,1)S(1)}, u32[]{:S(2)}, u32[]{:S(2)}) %collective-permute-start.4) | collective-permute-done | bytes 262176 | tf_op jit(solution)/shard_map/ppermute | solution.py:297
  45.0 1.1 %contract.5 = f32[512,256]{1,0:T(8,128)S(1)} custom-call(bf16[32,2,16,128]{3,2,1,0:T(8,128)(2,1)S(1)} %all_to_all.10.refs_0_, bf16[32,2,16,128]{3,2,1,0:T(8,128)(2,1)S(1)} %collective-permute-done.2.refs_0_.refs_1_, bf16[32,2,16,128]{3,2,1,0:T(8,128)(2,1)S(1)} %collective-permute-done.3.refs_1_.refs_2_, ...), custom_call_target="tpu_custom_call" | custom-call | tf_op jit(solution)/shard_map/contract/pallas_call | solution.py:349
  46.1 0.0 copy-start.2
  46.1 0.0 copy-start
  46.1 0.0 copy-start.1
  46.1 0.0 copy-start.3
  46.1 0.0 copy-start.4
  46.1 0.7 %convert_element_type.6 = f16[512,256]{1,0:T(8,128)(2,1)} convert(f32[512,256]{1,0:T(8,128)S(1)} %contract.5) | non-fusion elementwise | flops 131072 | bytes 786432 | tf_op jit(solution)/shard_map/convert_element_type | solution.py:365
  46.9 4.8 %all-to-all-start.1 = ((f16[32,16,256]{2,1,0:T(8,128)(2,1)}), f16[32,16,256]{2,1,0:T(8,128)(2,1)S(1)}, u32[]{:S(2)}, u32[]{:S(2)}) async-start(f16[32,16,256]{2,1,0:T(8,128)(2,1)} %bitcast.3), calls=%async_computation.1 | async-start | bytes 524288 | tf_op jit(solution)/shard_map/all_to_all | solution.py:364
  51.7 0.0 copy-done.2
  51.7 0.0 copy-done
  51.8 0.8 %prepare.1 = (f32[16,1200]{1,0:T(8,128)S(1)}, f32[16,1200]{1,0:T(8,128)S(1)}) custom-call(f32[16,1200]{1,0:T(8,128)S(1)} %copy-done.1, s32[1,1200]{1,0:T(1,128)S(1)} %get-tuple-element.18.vir_vec_ref, f32[1,1200]{1,0:T(1,128)S(1)} %reshape.12.energy_vec_ref, s32[128]{0:T(128)S(1)} %copy-done.3, s32[1200]{0:T(1024)S(1)} %copy-done, f32[128]{0:T(128)S(1)} %copy-done.4, ...), custom_call_target="tpu_custom_call" | custom-call | tf_op jit(solution)/shard_map/prepare/pallas_call | solution.py:372
  52.5 10.7 %all-to-all-done.1 = f16[32,16,256]{2,1,0:T(8,128)(2,1)S(1)} async-done(((f16[32,16,256]{2,1,0:T(8,128)(2,1)}), f16[32,16,256]{2,1,0:T(8,128)(2,1)S(1)}, u32[]{:S(2)}, u32[]{:S(2)}) %all-to-all-start.1) | async-done | bytes 262176 | tf_op jit(solution)/shard_map/all_to_all | solution.py:364
  63.3 0.6 %finish.1 = f32[16,1200]{1,0:T(8,128)} custom-call(f32[16,256]{1,0:T(8,128)S(1)} %convert_reduce_fusion.part_ref, f32[16,1200]{1,0:T(8,128)S(1)} %get-tuple-element.19.plain_ref, f32[16,1200]{1,0:T(8,128)S(1)} %get-tuple-element.20.factor_ref), custom_call_target="tpu_custom_call" | custom-call | tf_op jit(solution)/shard_map/finish/pallas_call | solution.py:388
  (6 shorter events, 0.1 us)
Async XLA Ops:
  1.5 2.0 %collective-permute-start = (bf16[2,64,16,128]{3,2,1,0:T(8,128)(2,1)S(1)}, bf16[2,64,16,128]{3,2,1,0:T(8,128)(2,1)S(1)}, u32[]{:S(2)}, u32[]{:S(2)}) collective-permute-start(bf16[2,64,16,128]{3,2,1,0:T(8,128)(2,1)S(1)} %fold_amplitudes.2.after_hbm), channel_id=1, source_target_pairs={{0,1},{1,0},{2,3},{3,2},{4,5},{5,4},{6,7},{7,6},{8,9},{9,8},{10,11... | collective-permute-start | bytes 1572872 | tf_op jit(solution)/shard_map/ppermute | solution.py:297
  3.6 9.9 %collective-permute-start.1 = (bf16[64,16,128]{2,1,0:T(8,128)(2,1)S(1)}, bf16[64,16,128]{2,1,0:T(8,128)(2,1)S(1)}, u32[]{:S(2)}, u32[]{:S(2)}) collective-permute-start(bf16[64,16,128]{2,1,0:T(8,128)(2,1)S(1)} %fusion.after_hbm), channel_id=1, source_target_pairs={{0,2},{1,3},{2,0},{3,1},{4,6},{5,7},{6,4},{7,5},{8,10},{9,11},{10,... | collective-permute-start | bytes 786440 | tf_op jit(solution)/shard_map/ppermute | solution.py:297
  9.1 34.8 %collective-permute-start.5 = (bf16[2,1200,256]{2,1,0:T(8,128)(2,1)S(1)}, bf16[2,1200,256]{2,1,0:T(8,128)(2,1)S(1)}, u32[]{:S(2)}, u32[]{:S(2)}) collective-permute-start(bf16[2,1200,256]{2,1,0:T(8,128)(2,1)S(1)} %get-tuple-element.13.refs_1_.refs_2_.refs_4_), channel_id=1, source_target_pairs={{0,192},{4,196},{8,200},{12,204},{16,208},{20,212},{24,216},{28,22... | collective-permute-start | bytes 3686408 | tf_op jit(solution)/shard_map/ppermute | solution.py:344
  35.5 7.9 %collective-permute-start.3 = (bf16[32,2,16,128]{3,2,1,0:T(8,128)(2,1)S(1)}, bf16[32,2,16,128]{3,2,1,0:T(8,128)(2,1)S(1)}, u32[]{:S(2)}, u32[]{:S(2)}) collective-permute-start(bf16[32,2,16,128]{3,2,1,0:T(8,128)(2,1)S(1)} %all_to_all.10.refs_0_), channel_id=1, source_target_pairs={{0,2},{1,3},{2,0},{3,1},{4,6},{5,7},{6,4},{7,5},{8,10},{9,11},{10,... | collective-permute-start | bytes 786440 | tf_op jit(solution)/shard_map/ppermute | solution.py:297
  36.3 7.1 %collective-permute-start.2 = (bf16[32,2,16,128]{3,2,1,0:T(8,128)(2,1)S(1)}, bf16[32,2,16,128]{3,2,1,0:T(8,128)(2,1)S(1)}, u32[]{:S(2)}, u32[]{:S(2)}) collective-permute-start(bf16[32,2,16,128]{3,2,1,0:T(8,128)(2,1)S(1)} %all_to_all.10.refs_0_), channel_id=1, source_target_pairs={{0,1},{1,0},{2,3},{3,2},{4,5},{5,4},{6,7},{7,6},{8,9},{9,8},{10,11... | collective-permute-start | bytes 786440 | tf_op jit(solution)/shard_map/ppermute | solution.py:297
  43.4 1.5 %collective-permute-start.4 = (bf16[32,2,16,128]{3,2,1,0:T(8,128)(2,1)S(1)}, bf16[32,2,16,128]{3,2,1,0:T(8,128)(2,1)S(1)}, u32[]{:S(2)}, u32[]{:S(2)}) collective-permute-start(bf16[32,2,16,128]{3,2,1,0:T(8,128)(2,1)S(1)} %collective-permute-done.3.refs_1_.refs_2_), channel_id=1, source_target_pairs={{0,1},{1,0},{2,3},{3,2},{4,5},{5,4},{6,7},{7,6},{8,9},{9,8},{10,11... | collective-permute-start | bytes 786440 | tf_op jit(solution)/shard_map/ppermute | solution.py:297
  46.1 5.6 %copy-start.2 = (f32[1200]{0:T(1024)S(1)}, f32[1200]{0:T(1024)}, u32[]{:S(2)}) copy-start(f32[1200]{0:T(1024)} %vir_e_ref.1) | copy-start | bytes 14404
  46.1 5.6 %copy-start = (s32[1200]{0:T(1024)S(1)}, s32[1200]{0:T(1024)}, u32[]{:S(2)}) copy-start(s32[1200]{0:T(1024)} %vir_ref.1) | copy-start | bytes 14404
  46.1 5.6 %copy-start.1 = (f32[16,1200]{1,0:T(8,128)S(1)}, f32[16,1200]{1,0:T(8,128)}, u32[]{:S(2)}) copy-start(f32[16,1200]{1,0:T(8,128)} %res_ref.1) | copy-start | bytes 230404
  46.1 5.6 %copy-start.3 = (s32[128]{0:T(128)S(1)}, s32[128]{0:T(128)}, u32[]{:S(2)}) copy-start(s32[128]{0:T(128)} %occ_ref.1) | copy-start | bytes 1540
  46.1 5.6 %copy-start.4 = (f32[128]{0:T(128)S(1)}, f32[128]{0:T(128)}, u32[]{:S(2)}) copy-start(f32[128]{0:T(128)} %occ_e_ref.1) | copy-start | bytes 1540
  46.9 16.4 %all-to-all-start.1 = ((f16[32,16,256]{2,1,0:T(8,128)(2,1)}), f16[32,16,256]{2,1,0:T(8,128)(2,1)S(1)}, u32[]{:S(2)}, u32[]{:S(2)}) async-start(f16[32,16,256]{2,1,0:T(8,128)(2,1)} %bitcast.3), calls=%async_computation.1 | async-start | bytes 524288 | tf_op jit(solution)/shard_map/all_to_all | solution.py:364
